TPU v7x, 32 devices: a whole 2x2x4 slice. The times are simulated.
32 devices in a mesh: fsdp: 8 (over y, x, core), sp: 4 (over z).
Axes of the slice: x: 2, y: 2, z: 4, core: 2. Of those that a mesh axis runs over, the one named last changes fastest.
Arguments:
- inputs: bfloat16 [8, 1536, 1024], P('fsdp', 'sp'), may hold values from -6 to 6
- segments: int32 [8, 1536], P('fsdp', 'sp'), may hold values from 0 to 4, as said below
- enc_states: bfloat16 [8, 1024, 1024], P('fsdp', 'sp'), may hold values from -6 to 6
- adapter_pick: int32 [8], P('fsdp'), may hold values from 0 to 7
- qkv_weights: bfloat16 [1, 6, 1024, 1024], P(None, None, 'fsdp'), may hold values from -0.1875 to 0.1875
- out_weights: bfloat16 [1, 2, 1024, 1024], P(None, None, 'fsdp'), may hold values from -0.75 to 0.75
- mlp_in: bfloat16 [1, 1024, 4096], P(None, 'fsdp'), may hold values from -0.1875 to 0.1875
- mlp_out: bfloat16 [1, 4096, 1024], P(None, 'fsdp'), may hold values from -0.09375 to 0.09375
- proj_down: bfloat16 [1, 8, 8, 16, 1024], replicated, may hold values from -0.1875 to 0.1875
- proj_up: bfloat16 [1, 8, 8, 16, 1024], replicated, may hold values from -0.75 to 0.75
- fc1_down: bfloat16 [1, 8, 16, 1024], replicated, may hold values from -0.1875 to 0.1875
- fc1_up: bfloat16 [1, 8, 16, 4096], replicated, may hold values from -0.75 to 0.75
- fc2_down: bfloat16 [1, 8, 16, 4096], replicated, may hold values from -0.09375 to 0.09375
- fc2_up: bfloat16 [1, 8, 16, 1024], replicated, may hold values from -0.75 to 0.75
- cotangent: bfloat16 [8, 1536, 1024], P('fsdp', 'sp'), may hold values from -6 to 6
Outputs:
- output: bfloat16 [8, 1536, 1024], P('fsdp', 'sp')
- input_grad: float32 [8, 1536, 1024], P('fsdp', 'sp')
- memory_grad: float32 [8, 1024, 1024], P('fsdp', 'sp')
- proj_down_grad: float32 [1, 8, 8, 16, 1024], replicated
- proj_up_grad: float32 [1, 8, 8, 16, 1024], replicated
- fc1_down_grad: float32 [1, 8, 16, 1024], replicated
- fc1_up_grad: float32 [1, 8, 16, 4096], replicated
- fc2_down_grad: float32 [1, 8, 16, 4096], replicated
- fc2_up_grad: float32 [1, 8, 16, 1024], replicated
Inputs may be any that keep to these rules, and one draw needn't show every extreme that they name: `segments`: segment numbers never fall along a sequence; segment 2 starts within the first 384 tokens of every sequence and ends within its last 384; the last token is in segment 4.
All inputs are finite; a program needn't handle non-finite values.
Results may differ from a plain program's by a relative error of at most 0.025.
The roundings to bfloat16 on the way count: a program that leaves them out, or rounds other values in their place, can miss the bound.
Values may be sent and summed in bfloat16 or wider, within the bound.
No kernel may reach another device: no remote copies, remote signals or barrier semaphores. Data moves between devices by JAX's collectives and lax.ppermute only.
A program may use at most 192 MiB of HBM per device.

v0:
```python
import functools

import jax
import jax.numpy as jnp
from jax import lax
from jax.experimental import pallas as pl
from jax.experimental.pallas import tpu as pltpu
from jax.sharding import Mesh
from jax.sharding import PartitionSpec as P

HEAD = 64
PAIR = 2 * HEAD
RANK = 16
AUG = 16
TERMS = 3
SEG_KINDS = 5
COLS = 256
NORM_EPS = 1e-05
FAR = -1e30
SCALE = HEAD**-0.5
F32 = jnp.float32
BF16 = jnp.bfloat16
ANY = pl.BlockSpec(memory_space=pltpu.HBM)
WHOLE = pl.BlockSpec(memory_space=pltpu.VMEM)


def dot(left, right, left_dim, right_dim):
    return lax.dot_general(left, right, (((left_dim,), (right_dim,)), ((), ())), preferred_element_type=F32)


def nn(left, right):
    return dot(left, right, 1, 0)


def nt(left, right):
    return dot(left, right, 1, 1)


def tn(left, right):
    return dot(left, right, 0, 0)


def params(mib):
    return pltpu.CompilerParams(vmem_limit_bytes=mib * 1024 * 1024)


def cost(us):
    return pl.CostEstimate(flops=int(us * 1.15e9), bytes_accessed=0, transcendentals=0)


def each(total, size, body, unroll=4):
    def step(at, carry):
        body(pl.ds(pl.multiple_of(at * size, size), size))
        return carry

    lax.fori_loop(0, total // size, step, 0, unroll=min(unroll, total // size))


def fetch(refs, layout, own, rows, part, target, sems):
    copies = []
    for ref, entries in zip(refs, layout):
        for source, flip, who, first, count in entries:
            low, high = max(first, part * rows), min(first + count, (part + 1) * rows)
            if low < high:
                shard = own ^ who if flip else who
                copies.append(
                    pltpu.make_async_copy(
                        ref.at[pl.ds(source + low - first, high - low)],
                        target.at[pl.ds(pl.multiple_of(shard * rows + (low - part * rows), 16), high - low)],
                        sems.at[len(copies)],
                    )
                )
    return copies


def start_all(copies):
    for copy in copies:
        copy.start()


def wait_all(copies):
    for copy in copies:
        copy.wait()


def low_half(shape, axis):
    return lax.broadcasted_iota(jnp.int32, shape, axis) < HEAD


def split_pair(rows):
    low = low_half(rows.shape, 1)
    zero = jnp.zeros_like(rows)
    return jnp.concatenate([jnp.where(low, rows, zero), jnp.where(low, zero, rows)], axis=0)


def split_pair_t(cols):
    low = low_half(cols.shape, 0)
    zero = jnp.zeros_like(cols)
    return jnp.concatenate([jnp.where(low, cols, zero), jnp.where(low, zero, cols)], axis=1)


def join_pair_t(cols):
    half = cols.shape[1] // 2
    return jnp.where(low_half((PAIR, half), 0), cols[:, :half], cols[:, half:])


def turned(rows):
    return rows.astype(F32).T


def term_rows(row, rest):
    high = row.astype(BF16).astype(F32)
    mid = (row - high).astype(BF16).astype(F32)
    low = row - high - mid
    at = lax.broadcasted_iota(jnp.int32, rest.shape, 0)
    return jnp.where(at == 0, high, jnp.where(at == 1, mid, jnp.where(at == 2, low, rest))).astype(BF16)


def causal_scores(scores):
    keys, columns = scores.shape
    row = lax.broadcasted_iota(jnp.int32, (keys, columns // 2), 0)
    col = lax.broadcasted_iota(jnp.int32, (keys, columns // 2), 1)
    keep = row <= col
    return jnp.where(jnp.concatenate([keep, keep], axis=1), scores, FAR)


def out_slopes(grads, outs):
    gt = turned(grads)
    products = gt * turned(outs)
    delta = jnp.concatenate([jnp.sum(products[:HEAD], axis=0, keepdims=True), jnp.sum(products[HEAD:], axis=0, keepdims=True)], axis=1)
    rest = jnp.zeros((AUG, delta.shape[1]), F32)
    return jnp.concatenate([split_pair_t(gt.astype(BF16)), term_rows(-delta, rest)], axis=0)


def block_back(keys, values, kaug, qa, ga, q, grads, diagonal):
    scores = nn(jnp.concatenate([keys, kaug], axis=1), qa)
    if diagonal:
        scores = causal_scores(scores)
    chances = jnp.exp(scores)
    slopes = nn(jnp.concatenate([values, kaug], axis=1), ga)
    low_slopes = (chances * slopes).astype(BF16)
    grad_values = nn(chances.astype(BF16), grads).astype(BF16)
    grad_keys = nn(low_slopes, q).astype(BF16)
    grad_q = join_pair_t(nn(turned(keys).astype(BF16), low_slopes))
    return grad_q, grad_keys, grad_values


def slope_rows(ga_ref, do_ref, o_ref):
    for at in range(ga_ref.shape[0]):
        cols = slice(at * PAIR, (at + 1) * PAIR)
        ga_ref[at] = out_slopes(do_ref[:, cols], o_ref[:, cols])


def adapter_spec(first, count, width):
    return pl.BlockSpec((1, count, 1, RANK, width), lambda *at: (0, first // count, at[-1][2], 0, 0))


def mlp_adapter_spec(width):
    return pl.BlockSpec((1, 1, RANK, width), lambda *at: (0, at[-1][2], 0, 0))


def low_rank(rows, table):
    return nt(rows, table).astype(BF16)


class Gathered:
    def __init__(self, arrays, layout, rows):
        self.arrays, self.layout, self.rows = arrays, layout, rows
        self.count = sum(len(entries) for entries in layout)

    def bring(self, refs, own, part, target, sems):
        return fetch(refs, self.layout, own, self.rows, part, target, sems)

    def specs(self):
        return [ANY] * len(self.arrays)

    def sems(self, parts):
        return pltpu.SemaphoreType.DMA((parts, self.count))


def project_into(out_ref, rows, weight, hidden, up):
    def body(cols):
        out_ref[:, cols] = (nn(rows, weight[:, cols]) + nn(hidden, up(cols))).astype(out_ref.dtype)

    each(out_ref.shape[1], COLS, body)


class Gathered:
    def __init__(self, arrays, layout, rows):
        self.arrays, self.layout, self.rows = arrays, layout, rows
        self.count = sum(len(entries) for entries in layout)

    def bring(self, refs, own, part, target, sems):
        return fetch(refs, self.layout, own, self.rows, part, target, sems)

    def specs(self):
        return [ANY] * len(self.arrays)

    def sems(self, parts):
        return pltpu.SemaphoreType.DMA((parts, self.count))


def project_into(out_ref, rows, weight, hidden, up):
    def body(cols):
        out_ref[:, cols] = (nn(rows, weight[:, cols]) + nn(hidden, up(cols))).astype(out_ref.dtype)

    each(out_ref.shape[1], COLS, body)


PER = 2


class Step:
    def __init__(self, name, w, parts, blocks, first, last, causal):
        self.name, self.w, self.parts, self.blocks, self.first, self.last, self.causal = name, w, parts, blocks, first, last, causal

    def on(self, sc_ref, at, condition=None):
        conditions = [] if condition is None else [condition]
        if self.causal and at:
            conditions.append(sc_ref[0] >= at)
        if not conditions:
            return lambda body: body()
        return pl.when(conditions[0] if len(conditions) == 1 else conditions[0] & conditions[1])


def head_cols(pair):
    return pl.ds(pl.multiple_of((pl.program_id(0) * PER + pair) * PAIR, PAIR), PAIR)


def pair_cols(pair):
    return slice(pair * PAIR, (pair + 1) * PAIR)


def attend_step_kernel(step, counts, sc_ref, *refs):
    refs = list(refs)
    make_q = step.causal and step.first

    def take(number):
        return [refs.pop(0) for _ in range(number)]

    groups = len(counts)
    xs = [take(count) for count in counts]
    kaugs = take(groups)
    a_ref, b_ref = take(2)
    q_ref = take(1)[0] if step.first and not make_q else None
    seg_ref = take(1)[0] if step.first else None
    qa_in, acc_in, m_in = (None, None, None) if step.first else take(3)
    pieces = take(len(step.w.arrays))
    q_out = take(1)[0] if make_q else None
    k_outs, v_outs, r_outs = take(groups), take(groups), take(groups)
    qa_out, o_out = None, None
    if step.first and not step.last:
        qa_out = take(1)[0]
    if step.last:
        o_out, qa_out, w_ref, sems = take(4)
    else:
        acc_ref, m_ref, w_ref, sems = take(4)
    k_alls, v_alls = take(groups), take(groups)
    if step.last:
        acc_ref, m_ref = take(2)
    q_all = take(1)[0] if make_q else None
    parts = step.parts

    def copies(at):
        return step.w.bring(pieces, sc_ref[1], parts[at], w_ref.at[at], sems.at[at])

    for group, at in enumerate(step.blocks):

        @step.on(sc_ref, at, pl.program_id(0) == 0)
        def _(group=group):
            if group == 0:
                for slot in range(len(parts)):
                    start_all(copies(slot))
            low = 0
            tables = a_ref[...].reshape(-1, a_ref.shape[-1])
            for x_ref in xs[group]:
                x = x_ref[...]
                span = pl.ds(low, x.shape[0])
                low += x.shape[0]
                hidden = low_rank(x, tables)
                r_outs[group][span, :] = hidden
                outs = [k_alls[group], v_alls[group]]
                if make_q and group == 0:
                    outs.insert(0, q_all)
                for number, out in enumerate(outs):
                    place = number + len(parts) - len(outs)
                    slot = number + a_ref.shape[1] - len(outs)
                    own = hidden[:, slot * RANK : (slot + 1) * RANK]
                    if group == 0 and x_ref is xs[0][0]:
                        wait_all(copies(place))

                    def body(cols, place=place, slot=slot, own=own, out=out):
                        out[span, cols] = (nn(x, w_ref[place, :, cols]) + nn(own, b_ref[0, slot, 0, :, cols])).astype(BF16)

                    each(out.shape[1], COLS, body)

    qas = []
    for pair in range(PER):
        if step.first:
            q = q_all[:, head_cols(pair)] if make_q else q_ref[:, pair_cols(pair)]
            if make_q:
                q_out[:, pair_cols(pair)] = q
            seg = seg_ref[...]
            qt = split_pair_t((turned(q) * SCALE).astype(BF16))
            qas.append(jnp.concatenate([qt, jnp.concatenate([seg, seg], axis=1).astype(BF16)], axis=0))
            if not step.last:
                qa_out[pair] = qas[pair]
        else:
            qas.append(qa_in[pair])

    def block(group, at, opens):
        for pair in range(PER):
            keys, values = k_alls[group][:, head_cols(pair)], v_alls[group][:, head_cols(pair)]
            k_outs[group][:, pair_cols(pair)] = keys
            v_outs[group][:, pair_cols(pair)] = values
            scores = nn(jnp.concatenate([keys, kaugs[group][...]], axis=1), qas[pair])
            if step.causal and at == 0:
                scores = causal_scores(scores)
            top = jnp.max(scores, axis=0, keepdims=True)
            vt = jnp.concatenate([turned(values).astype(BF16), jnp.ones((16, keys.shape[0]), BF16)], axis=0)
            if opens and step.first:
                acc_ref[pair] = nn(vt, jnp.exp(scores - top).astype(BF16))
            else:
                old = m_in[pair, 0:1] if opens else m_ref[pair, 0:1]
                so_far = acc_in[pair] if opens else acc_ref[pair]
                top = jnp.maximum(old, top)
                acc_ref[pair] = so_far * jnp.exp(old - top) + nn(vt, jnp.exp(scores - top).astype(BF16))
            m_ref[pair] = jnp.broadcast_to(top, m_ref.shape[1:])

    for group, at in enumerate(step.blocks):
        step.on(sc_ref, at)(functools.partial(block, group, at, group == 0))
    if step.causal and step.blocks[0]:

        @pl.when(sc_ref[0] < step.blocks[0])
        def _():
            acc_ref[...] = acc_in[...]
            m_ref[...] = m_in[...]

    if step.last:
        for pair in range(PER):
            total = acc_ref[pair, PAIR : PAIR + 1]
            o_out[:, pair_cols(pair)] = join_pair_t(acc_ref[pair, :PAIR] / total).T.astype(BF16)
            lse = m_ref[pair, 0:1] + jnp.log(total)
            qa_out[pair] = jnp.concatenate([qas[pair][:PAIR], term_rows(-lse, qas[pair][PAIR:].astype(F32))], axis=0)


def attend_step(step, scalars, xs, tokens, block_rows, tables, kaugs, q, seg, state):
    width = xs[0][0].shape[1]
    pairs = width // PAIR
    keys = [block_rows * len(group) for group in xs]
    make_q = step.causal and step.first
    kinds = len(step.parts)
    slots = 3 if step.causal else 2
    by_head = pl.BlockSpec((tokens, PER * PAIR), lambda h, s: (0, h))
    extended = pl.BlockSpec((PER, PAIR + AUG, 2 * tokens), lambda h, s: (h, 0, 0))
    m_spec = pl.BlockSpec((PER, 8, 2 * tokens), lambda h, s: (h, 0, 0))
    adapters = adapter_spec(0 if step.causal else 4, slots, width)
    q_shape = jax.ShapeDtypeStruct((tokens, width), BF16)
    qa_shape = jax.ShapeDtypeStruct((pairs, PAIR + AUG, 2 * tokens), BF16)
    in_specs = [pl.BlockSpec((block_rows, width), lambda h, s: (0, 0))] * sum(len(group) for group in xs)
    in_specs += [pl.BlockSpec((rows, AUG), lambda h, s: (0, 0)) for rows in keys] + [adapters, adapters]
    args = [x for group in xs for x in group] + [*kaugs, *tables]
    if step.first and not make_q:
        in_specs.append(by_head)
        args.append(q)
    if step.first:
        in_specs.append(pl.BlockSpec((AUG, tokens), lambda h, s: (0, 0)))
        args.append(seg)
    else:
        in_specs += [extended, extended, m_spec]
        args += state
    keys_by_head = [pl.BlockSpec((rows, PER * PAIR), lambda h, s: (0, h)) for rows in keys]
    out_specs = [*keys_by_head, *keys_by_head, *[pl.BlockSpec((rows, slots * RANK), lambda h, s: (0, 0)) for rows in keys]]
    kv_shapes = [jax.ShapeDtypeStruct((rows, width), BF16) for rows in keys]
    out_shape = [*kv_shapes, *kv_shapes, *[jax.ShapeDtypeStruct((rows, slots * RANK), BF16) for rows in keys]]
    if make_q:
        out_specs.insert(0, by_head)
        out_shape.insert(0, q_shape)
    scratch = [pltpu.VMEM((kinds, width, width), BF16), step.w.sems(kinds)]
    scratch += [pltpu.VMEM((rows, width), BF16) for rows in keys] * 2
    state_shapes = [(PAIR + 16, 2 * tokens), (8, 2 * tokens)]
    if step.first and not step.last:
        out_specs.append(extended)
        out_shape.append(qa_shape)
    if step.last:
        out_specs += [by_head, extended]
        out_shape += [q_shape, qa_shape]
        scratch += [pltpu.VMEM((PER, *shape), F32) for shape in state_shapes]
    else:
        out_specs += [extended, m_spec]
        out_shape += [jax.ShapeDtypeStruct((pairs, *shape), F32) for shape in state_shapes]
    if make_q:
        scratch.append(pltpu.VMEM((tokens, width), BF16))
    call = pl.pallas_call(
        functools.partial(attend_step_kernel, step, [len(group) for group in xs]),
        grid_spec=pltpu.PrefetchScalarGridSpec(
            num_scalar_prefetch=1, grid=(pairs // PER,), in_specs=in_specs + step.w.specs(), out_specs=out_specs, scratch_shapes=scratch
        ),
        out_shape=out_shape,
        name=step.name,
        compiler_params=params(60),
        cost_estimate=cost(sum(keys) / 32),
    )
    out = list(call(scalars, *args, *step.w.arrays))
    q = out.pop(0) if make_q else q
    count = len(xs)
    return q, out[:count], out[count : 2 * count], out[2 * count : 3 * count], out[3 * count :]


def back_step_kernel(step, count, sc_ref, *refs):
    refs = list(refs)

    def take(number):
        return [refs.pop(0) for _ in range(number)]

    qa_ref, ga_ref, q_ref, do_ref, k_ref, v_ref, kaug_ref, r_ref, a_ref, b_ref = take(10)
    xs = take(count)
    dqt_in, sums_in = (None, None) if step.first else take(2)
    query = step.causal and step.last
    d1_ref = take(1)[0] if query else None
    pieces = take(len(step.w.arrays))
    dq_all = None
    if query:
        base_ref, grads_ref, w_ref, dk_all, dv_all, sems, dq_all = refs
    elif step.last:
        own_ref, part_ref, dq_ref, grads_ref, w_ref, dk_all, dv_all, sems = refs
    else:
        part_ref, dqt_ref, sums_ref, w_ref, dk_all, dv_all, sems = refs
    h = pl.program_id(0)
    final = h == pl.num_programs(0) - 1
    width = a_ref.shape[-1]
    parts = step.parts
    slots = a_ref.shape[1]
    keys = k_ref.shape[0]
    block = min(keys, 512)
    (at,) = step.blocks

    def weights():
        return [step.w.bring(pieces, sc_ref[1], part, w_ref.at[place], sems.at[place]) for place, part in enumerate(parts)]

    @step.on(sc_ref, at, h == 0)
    def _():
        for part in weights():
            start_all(part)

    @step.on(sc_ref, at)
    def _():
        for pair in range(PER):
            cols, all_cols = pair_cols(pair), head_cols(pair)
            q = split_pair(q_ref[:, cols] * jnp.asarray(SCALE, BF16))
            grads = split_pair(do_ref[:, cols])
            total = None
            for low in range(0, keys, block):
                span = slice(low, low + block)
                grad_q, grad_keys, grad_values = block_back(
                    k_ref[span, cols], v_ref[span, cols], kaug_ref[span], qa_ref[pair], ga_ref[pair], q, grads, step.causal and at == 0
                )
                dk_all[span, all_cols] = grad_keys
                dv_all[span, all_cols] = grad_values
                total = grad_q if total is None else total + grad_q
            if not step.first:
                total = total + dqt_in[pair]
            if query:
                dq_all[:, all_cols] = (total * SCALE).T.astype(BF16)
            elif step.last:
                dq_ref[:, cols] = (total * SCALE).T.astype(BF16)
            else:
                dqt_ref[pair] = total

    if step.causal and at:

        @pl.when(sc_ref[0] < at)
        def _():
            dqt_ref[...] = jnp.zeros_like(dqt_ref[...]) if step.first else dqt_in[...]

            @pl.when(final)
            def _():
                part_ref[...] = jnp.zeros_like(part_ref)
                sums_ref[...] = jnp.zeros_like(sums_ref) if step.first else sums_in[...]

    @step.on(sc_ref, at, final)
    def _():
        grads = [dq_all, dk_all, dv_all] if query else [dk_all, dv_all]
        shift = slots - len(grads)
        drs, dbs = [], []
        hidden = r_ref[...]
        for place, grad_ref in enumerate(grads):
            slot = place + shift
            grad = grad_ref[...]
            drs.append(low_rank(grad, b_ref[0, slot, 0]))
            dbs.append(tn(hidden[:, slot * RANK : (slot + 1) * RANK], grad))
        dr = jnp.concatenate(drs, axis=1)
        low, da = 0, None
        for x_ref in xs:
            part = tn(dr[low : low + x_ref.shape[0]], x_ref[...])
            da = part if da is None else da + part
            low += x_ref.shape[0]
        olds = [None] * 4 if step.first else [sums_in[place * RANK : (place + 1) * RANK] for place in range(4)]
        if query:
            olds = [None, *olds[:2], None, *olds[2:]]
        total = [da[place * RANK : (place + 1) * RANK] for place in range(len(grads))] + dbs
        target = grads_ref if step.last else sums_ref
        for place, (new, old) in enumerate(zip(total, olds)):
            target[place * RANK : (place + 1) * RANK] = (new if old is None else new + old).astype(target.dtype)
        for part in weights():
            wait_all(part)
        own = keys // count if step.last and not query else 0

        def body(cols):
            table = a_ref[0, shift:, 0, :, cols].reshape(len(grads) * RANK, COLS)
            value = nn(dr, table)
            for place, grad_ref in enumerate(grads):
                value = value + nt(grad_ref[...], w_ref[place, cols, :])
            if query:
                base_ref[:, cols] = value + d1_ref[:, cols]
            elif step.last:
                own_ref[:, cols] = value[:own]
                part_ref[:, cols] = value[own:].astype(BF16)
            else:
                part_ref[:, cols] = value.astype(BF16)

        each(width, COLS, body)


def back_step(step, scalars, qa, ga, q, do, k, v, kaug, r, xs, block_rows, tables, state, d1):
    tokens, width = q.shape
    pairs = width // PAIR
    keys = k.shape[0]
    slots = 3 if step.causal else 2
    query = step.causal and step.last
    by_head = pl.BlockSpec((tokens, PER * PAIR), lambda h, s: (0, h))
    keys_by_head = pl.BlockSpec((keys, PER * PAIR), lambda h, s: (0, h))
    extended = pl.BlockSpec((PER, PAIR + AUG, 2 * tokens), lambda h, s: (h, 0, 0))
    dqt_spec = pl.BlockSpec((PER, PAIR, tokens), lambda h, s: (h, 0, 0))

    def whole(rows):
        return pl.BlockSpec((rows, width), lambda h, s: (0, 0))

    adapters = adapter_spec(0 if step.causal else 4, slots, width)
    in_specs = [
        extended,
        extended,
        by_head,
        by_head,
        keys_by_head,
        keys_by_head,
        pl.BlockSpec((keys, AUG), lambda h, s: (0, 0)),
        pl.BlockSpec((keys, slots * RANK), lambda h, s: (0, 0)),
        adapters,
        adapters,
        *[whole(block_rows)] * len(xs),
    ]
    args = [qa, ga, q, do, k, v, kaug, r, *tables, *xs]
    if not step.first:
        in_specs += [dqt_spec, whole(4 * RANK)]
        args += state
    scratch = [pltpu.VMEM((len(step.parts), width, width), BF16), pltpu.VMEM((keys, width), BF16), pltpu.VMEM((keys, width), BF16)]
    scratch.append(step.w.sems(len(step.parts)))
    if query:
        in_specs.append(whole(tokens))
        args.append(d1)
        scratch.append(pltpu.VMEM((tokens, width), BF16))
        out_specs = [whole(tokens), whole(6 * RANK)]
        out_shape = [jax.ShapeDtypeStruct((tokens, width), F32), jax.ShapeDtypeStruct((6 * RANK, width), BF16)]
    elif step.last:
        rest = keys - block_rows
        out_specs = [whole(block_rows), whole(rest), by_head, whole(4 * RANK)]
        out_shape = [
            jax.ShapeDtypeStruct((block_rows, width), F32),
            jax.ShapeDtypeStruct((rest, width), BF16),
            jax.ShapeDtypeStruct((tokens, width), BF16),
            jax.ShapeDtypeStruct((4 * RANK, width), BF16),
        ]
    else:
        out_specs = [whole(keys), dqt_spec, whole(4 * RANK)]
        out_shape = [
            jax.ShapeDtypeStruct((keys, width), BF16),
            jax.ShapeDtypeStruct((pairs, PAIR, tokens), F32),
            jax.ShapeDtypeStruct((4 * RANK, width), F32),
        ]
    return pl.pallas_call(
        functools.partial(back_step_kernel, step, len(xs)),
        grid_spec=pltpu.PrefetchScalarGridSpec(
            num_scalar_prefetch=1, grid=(pairs // PER,), in_specs=in_specs + step.w.specs(), out_specs=out_specs, scratch_shapes=scratch
        ),
        out_shape=out_shape,
        name=step.name,
        compiler_params=params(60),
        cost_estimate=cost(keys / 24),
    )(scalars, *args, *step.w.arrays)


ROWS = 64


def normalize_rows(u_ref, norm_ref, low_ref, std_ref):
    def body(rows):
        values = u_ref[rows, :]
        centered = values - jnp.mean(values, -1, keepdims=True)
        inv_std = lax.rsqrt(jnp.mean(centered * centered, -1, keepdims=True) + NORM_EPS)
        normed = centered * inv_std
        norm_ref[rows, :] = normed
        low_ref[rows, :] = normed.astype(BF16)
        std_ref[rows, :] = inv_std

    each(u_ref.shape[0], ROWS, body)


def normalize_back(grads, normed, inv_std):
    return inv_std * (grads - jnp.mean(grads, -1, keepdims=True) - normed * jnp.mean(grads * normed, -1, keepdims=True))


def mid_kernel(w, part, query, sc_ref, o_ref, x_ref, a_ref, b_ref, aq_ref, bq_ref, *refs):
    pieces, refs = refs[: len(w.arrays)], refs[len(w.arrays) :]
    if query:
        norm_ref, low_ref, std_ref, r_ref, q_ref, w_ref, u_ref, sems = refs
    else:
        norm_ref, low_ref, std_ref, r_ref, w_ref, u_ref, sems = refs
    width = x_ref.shape[1]
    first = w.bring(pieces, sc_ref[1], part, w_ref.at[0], sems.at[0])
    start_all(first)
    if query:
        second = w.bring(pieces, sc_ref[1], 2, w_ref.at[1], sems.at[1])
        start_all(second)
    o = o_ref[...]
    hidden = low_rank(o, a_ref[0, 0, 0])
    r_ref[:, :RANK] = hidden
    wait_all(first)

    def body(cols):
        u_ref[:, cols] = x_ref[:, cols].astype(F32) + nn(o, w_ref[0, :, cols]) + nn(hidden, b_ref[0, 0, 0, :, cols])

    each(width, COLS, body)
    normalize_rows(u_ref, norm_ref, low_ref, std_ref)
    if query:
        low = low_ref[...]
        hidden_q = low_rank(low, aq_ref[0, 0, 0])
        r_ref[:, RANK:] = hidden_q
        wait_all(second)
        project_into(q_ref, low, w_ref.at[1], hidden_q, lambda cols: bq_ref[0, 0, 0, :, cols])


def mid(name, scalars, outs, residual, part, proj, query, proj_down, proj_up, w):
    rows, width = outs.shape
    shapes = [
        jax.ShapeDtypeStruct((rows, width), F32),
        jax.ShapeDtypeStruct((rows, width), BF16),
        jax.ShapeDtypeStruct((rows, 1), F32),
        jax.ShapeDtypeStruct((rows, 2 * RANK if query else RANK), BF16),
    ]
    if query:
        shapes.append(jax.ShapeDtypeStruct((rows, width), BF16))
    spec, spec_q = adapter_spec(proj, 1, width), adapter_spec(3, 1, width)
    return pl.pallas_call(
        functools.partial(mid_kernel, w, part, query),
        grid_spec=pltpu.PrefetchScalarGridSpec(
            num_scalar_prefetch=1,
            grid=(1,),
            in_specs=[WHOLE, WHOLE, spec, spec, spec_q, spec_q, *w.specs()],
            out_specs=[WHOLE] * len(shapes),
            scratch_shapes=[pltpu.VMEM((2, width, width), BF16), pltpu.VMEM((rows, width), F32), w.sems(2)],
        ),
        out_shape=shapes,
        name=name,
        compiler_params=params(60),
        cost_estimate=cost(1),
    )(scalars, outs, residual, proj_down, proj_up, proj_down, proj_up, *w.arrays)


def gelu_kernel(w, sc_ref, x_ref, a_ref, b_ref, *refs):
    pieces, (g_ref, slope_ref, r_ref, w_ref, sems) = refs[: len(w.arrays)], refs[len(w.arrays) :]
    copies = w.bring(pieces, sc_ref[1], 0, w_ref, sems.at[0])
    start_all(copies)
    x = x_ref[...]
    hidden = low_rank(x, a_ref[0, 0])
    r_ref[...] = hidden
    wait_all(copies)

    def body(cols):
        pre = nn(x, w_ref[:, cols]) + nn(hidden, b_ref[0, 0, :, cols])
        phi = 0.5 * (1.0 + lax.erf(pre * 0.7071067811865476))
        g_ref[:, cols] = (pre * phi).astype(BF16)
        slope_ref[:, cols] = (phi + pre * jnp.exp(-0.5 * pre * pre) * 0.3989422804014327).astype(BF16)

    each(g_ref.shape[1], COLS, body)


def gelu_up(scalars, x, down, up, w):
    rows, width = x.shape
    wide = up.shape[3]
    return pl.pallas_call(
        functools.partial(gelu_kernel, w),
        grid_spec=pltpu.PrefetchScalarGridSpec(
            num_scalar_prefetch=1,
            grid=(1,),
            in_specs=[WHOLE, mlp_adapter_spec(width), mlp_adapter_spec(wide), *w.specs()],
            out_specs=[WHOLE] * 3,
            scratch_shapes=[pltpu.VMEM((width, wide), BF16), w.sems(1)],
        ),
        out_shape=[
            jax.ShapeDtypeStruct((rows, wide), BF16),
            jax.ShapeDtypeStruct((rows, wide), BF16),
            jax.ShapeDtypeStruct((rows, RANK), BF16),
        ],
        name="gelu_up",
        compiler_params=params(60),
        cost_estimate=cost(15),
    )(scalars, x, down, up, *w.arrays)


FC_ROWS = {"da1": 0, "db1": 16, "da2": 80, "db2": 144, "da_co": 160, "db_co": 176, "pick": 192}
FC_TOTAL = 208


def mlp_kernel(w_up, w_down, w_mid, sc_ref, g_ref, slope_ref, h2_ref, h2_low_ref, std2_ref, cot_ref, r1_ref, rco_ref, oc_ref,
               a1_ref, b1_ref, a2_ref, b2_ref, a7_ref, b7_ref, *refs):
    ups, refs = refs[: len(w_up.arrays)], refs[len(w_up.arrays) :]
    downs, refs = refs[: len(w_down.arrays)], refs[len(w_down.arrays) :]
    mids, refs = refs[: len(w_mid.arrays)], refs[len(w_mid.arrays) :]
    y_ref, d2_ref, doc_ref, gac_ref, grads_ref, w1, w2, wco, u, low, dpre, sem1, sem2, sem3 = refs
    rows, width = h2_ref.shape
    wide = g_ref.shape[1]
    own = sc_ref[1]
    copies2 = w_down.bring(downs, own, 0, w2, sem2.at[0])
    copies1 = w_up.bring(ups, own, 0, w1, sem1.at[0])
    copies3 = w_mid.bring(mids, own, 1, wco, sem3.at[0])
    start_all(copies2)
    start_all(copies1)
    start_all(copies3)
    g = g_ref[...]
    r2 = low_rank(g, a2_ref[0, 0])
    wait_all(copies2)

    def second(cols):
        u[:, cols] = h2_ref[:, cols] + nn(g_ref[...], w2[:, cols]) + nn(r2, b2_ref[0, 0, :, cols])

    each(width, COLS, second)

    def third(at):
        values = u[at, :]
        centered = values - jnp.mean(values, -1, keepdims=True)
        inv_std = lax.rsqrt(jnp.mean(centered * centered, -1, keepdims=True) + NORM_EPS)
        normed = centered * inv_std
        y_ref[at, :] = normed.astype(BF16)
        d3 = normalize_back(cot_ref[at, :].astype(F32), normed, inv_std)
        u[at, :] = d3
        low[at, :] = d3.astype(BF16)

    each(rows, ROWS, third)
    d3_low = low[...]
    grads_ref[pl.ds(FC_ROWS["db2"], RANK), :] = tn(r2, d3_low).astype(BF16)
    dr2 = low_rank(d3_low, b2_ref[0, 0])
    r1 = r1_ref[...]
    run = 2 * COLS
    runs = width // run

    def slopes(at, carry):
        cols = pl.ds(pl.multiple_of(at * run, run), run)
        down_rows = nt(low[...], w2[cols, :]) + nn(dr2, a2_ref[0, 0, :, cols])
        part = (down_rows * slope_ref[:, cols].astype(F32)).astype(BF16)
        dpre[:, cols] = part
        row = pl.multiple_of((at // runs) * RANK, RANK)
        place = pl.ds(pl.multiple_of((at % runs) * run, run), run)
        grads_ref[pl.ds(FC_ROWS["da2"] + row, RANK), place] = tn(dr2, g_ref[:, cols]).astype(BF16)
        grads_ref[pl.ds(FC_ROWS["db1"] + row, RANK), place] = tn(r1, part).astype(BF16)
        return carry

    lax.fori_loop(0, wide // run, slopes, 0)
    dr1 = low_rank(dpre[...], b1_ref[0, 0])
    grads_ref[pl.ds(FC_ROWS["da1"], RANK), :] = tn(dr1, h2_low_ref[...]).astype(BF16)
    wait_all(copies1)

    def first(cols):
        u[:, cols] += nt(dpre[...], w1[cols, :]) + nn(dr1, a1_ref[0, 0, :, cols])

    each(width, COLS, first)

    def norm(at):
        d2 = normalize_back(u[at, :], h2_ref[at, :], std2_ref[at, :])
        d2_ref[at, :] = d2
        low[at, :] = d2.astype(BF16)

    each(rows, ROWS, norm)
    wait_all(copies3)
    d2_low = low[...]
    grads_ref[pl.ds(FC_ROWS["db_co"], RANK), :] = tn(rco_ref[...], d2_low).astype(BF16)
    drc = low_rank(d2_low, b7_ref[0, 0, 0])
    grads_ref[pl.ds(FC_ROWS["da_co"], RANK), :] = tn(drc, oc_ref[...]).astype(BF16)

    def cross(cols):
        doc_ref[:, cols] = (nt(low[...], wco[cols, :]) + nn(drc, a7_ref[0, 0, 0, :, cols])).astype(BF16)

    each(width, COLS, cross)
    slope_rows(gac_ref, doc_ref, oc_ref)
    mine = jnp.where(sc_ref[0] == 0, sc_ref[2], 0).astype(F32)
    grads_ref[pl.ds(FC_ROWS["pick"], 16), :] = jnp.full((16, width), mine, F32).astype(BF16)


def mlp(scalars, g, slope, h2, h2_low, std2, cot, r1, rco, oc, fc1_down, fc1_up, fc2_down, fc2_up, proj_down, proj_up, w_up, w_down, w_mid):
    rows, width = h2.shape
    wide = g.shape[1]
    return pl.pallas_call(
        functools.partial(mlp_kernel, w_up, w_down, w_mid),
        grid_spec=pltpu.PrefetchScalarGridSpec(
            num_scalar_prefetch=1,
            grid=(1,),
            in_specs=[
                *[WHOLE] * 9,
                mlp_adapter_spec(width),
                mlp_adapter_spec(wide),
                mlp_adapter_spec(wide),
                mlp_adapter_spec(width),
                adapter_spec(7, 1, width),
                adapter_spec(7, 1, width),
                *w_up.specs(),
                *w_down.specs(),
                *w_mid.specs(),
            ],
            out_specs=[WHOLE] * 5,
            scratch_shapes=[
                pltpu.VMEM((width, wide), BF16),
                pltpu.VMEM((wide, width), BF16),
                pltpu.VMEM((width, width), BF16),
                pltpu.VMEM((rows, width), F32),
                pltpu.VMEM((rows, width), BF16),
                pltpu.VMEM((rows, wide), BF16),
                w_up.sems(1),
                w_down.sems(1),
                w_mid.sems(1),
            ],
        ),
        out_shape=[
            jax.ShapeDtypeStruct((rows, width), BF16),
            jax.ShapeDtypeStruct((rows, width), F32),
            jax.ShapeDtypeStruct((rows, width), BF16),
            jax.ShapeDtypeStruct((width // PAIR, PAIR + AUG, 2 * rows), BF16),
            jax.ShapeDtypeStruct((FC_TOTAL, width), BF16),
        ],
        name="mlp",
        compiler_params=params(60),
        cost_estimate=cost(33),
    )(scalars, g, slope, h2, h2_low, std2, cot, r1, rco, oc, fc1_down, fc1_up, fc2_down, fc2_up, proj_down, proj_up,
      *w_up.arrays, *w_down.arrays, *w_mid.arrays)


def mid_back_kernel(w, sc_ref, dqc_ref, d2_ref, h1_ref, h1_low_ref, std1_ref, r_ref, o_ref, aq_ref, bq_ref, a_ref, b_ref, *refs):
    pieces, refs = refs[: len(w.arrays)], refs[len(w.arrays) :]
    d1_ref, do_ref, ga_ref, grads_ref, w_ref, low, sems = refs
    rows, width = d2_ref.shape
    first = w.bring(pieces, sc_ref[1], 2, w_ref.at[1], sems.at[1])
    second = w.bring(pieces, sc_ref[1], 0, w_ref.at[0], sems.at[0])
    start_all(first)
    start_all(second)
    dqc = dqc_ref[...]
    drq = low_rank(dqc, bq_ref[0, 0, 0])
    grads_ref[0:RANK, :] = tn(drq, h1_low_ref[...]).astype(BF16)
    grads_ref[2 * RANK : 3 * RANK, :] = tn(r_ref[:, RANK:], dqc).astype(BF16)
    wait_all(first)

    def query(cols):
        d1_ref[:, cols] = d2_ref[:, cols] + nt(dqc_ref[...], w_ref[1, cols, :]) + nn(drq, aq_ref[0, 0, 0, :, cols])

    each(width, COLS, query)

    def norm(at):
        d1 = normalize_back(d1_ref[at, :], h1_ref[at, :], std1_ref[at, :])
        d1_ref[at, :] = d1
        low[at, :] = d1.astype(BF16)

    each(rows, ROWS, norm)
    wait_all(second)
    d1_low = low[...]
    dr = low_rank(d1_low, b_ref[0, 0, 0])
    grads_ref[RANK : 2 * RANK, :] = tn(dr, o_ref[...]).astype(BF16)
    grads_ref[3 * RANK :, :] = tn(r_ref[:, :RANK], d1_low).astype(BF16)

    def out(cols):
        do_ref[:, cols] = (nt(low[...], w_ref[0, cols, :]) + nn(dr, a_ref[0, 0, 0, :, cols])).astype(BF16)

    each(width, COLS, out)

    slope_rows(ga_ref, do_ref, o_ref)


def mid_back(scalars, dqc, d2, h1, h1_low, std1, r, o, proj_down, proj_up, w):
    rows, width = d2.shape
    spec, spec_q = adapter_spec(6, 1, width), adapter_spec(3, 1, width)
    return pl.pallas_call(
        functools.partial(mid_back_kernel, w),
        grid_spec=pltpu.PrefetchScalarGridSpec(
            num_scalar_prefetch=1,
            grid=(1,),
            in_specs=[*[WHOLE] * 7, spec_q, spec_q, spec, spec, *w.specs()],
            out_specs=[WHOLE] * 4,
            scratch_shapes=[pltpu.VMEM((2, width, width), BF16), pltpu.VMEM((rows, width), BF16), w.sems(2)],
        ),
        out_shape=[
            jax.ShapeDtypeStruct((rows, width), F32),
            jax.ShapeDtypeStruct((rows, width), BF16),
            jax.ShapeDtypeStruct((width // PAIR, PAIR + AUG, 2 * rows), BF16),
            jax.ShapeDtypeStruct((4 * RANK, width), BF16),
        ],
        name="mid_back",
        compiler_params=params(60),
        cost_estimate=cost(1),
    )(scalars, dqc, d2, h1, h1_low, std1, r, o, proj_down, proj_up, proj_down, proj_up, *w.arrays)


def add_picked(picks_ref, sequences, out, source):
    adapters, view = out
    for adapter in range(adapters):
        view(adapter)[...] = jnp.zeros(view(adapter).shape, F32)
    for at in range(sequences):
        target = view(picks_ref[at])
        target[...] += source(at).astype(F32)


def fc_total_kernel(picks_ref, g_ref, a1_ref, b1_ref, a2_ref, b2_ref):
    sequences, _, width = g_ref.shape
    adapters = a1_ref.shape[1]

    def put(out_ref, col, row):
        def view(adapter):
            return out_ref.at[0, adapter, :, pl.ds(col, width)]

        add_picked(picks_ref, sequences, (adapters, view), lambda at: g_ref[at, pl.ds(row, RANK), :])

    for out_ref, name in ((a1_ref, "da1"), (b1_ref, "db1"), (a2_ref, "da2"), (b2_ref, "db2")):
        for at in range(out_ref.shape[3] // width):
            put(out_ref, at * width, FC_ROWS[name] + at * RANK)


def fc_total(picks, gathered, shapes):
    return pl.pallas_call(
        fc_total_kernel,
        grid_spec=pltpu.PrefetchScalarGridSpec(
            num_scalar_prefetch=1, grid=(1,), in_specs=[WHOLE], out_specs=[WHOLE] * 4
        ),
        out_shape=[jax.ShapeDtypeStruct(s, F32) for s in shapes],
        name="fc_total",
        compiler_params=params(60),
        cost_estimate=cost(6),
    )(picks, gathered)


PROJ_ROWS = {
    0: (2, 0, 48),
    1: (2, 16, 64),
    2: (2, 32, 80),
    3: (1, 0, 32),
    4: (1, 64, 96),
    5: (1, 80, 112),
    6: (1, 16, 48),
    7: (0, FC_ROWS["da_co"], FC_ROWS["db_co"]),
}


def proj_total_kernel(projs, first_source, count, sources, picks_ref, *refs):
    g_refs, (down_ref, up_ref) = refs[:sources], refs[-2:]
    adapters = down_ref.shape[2]
    for at, proj in enumerate(projs):
        source, down_row, up_row = PROJ_ROWS[proj]
        g_ref = g_refs[source - first_source]

        @pl.when(pl.program_id(0) == at)
        def _(g_ref=g_ref, down_row=down_row, up_row=up_row):
            for out_ref, row in ((down_ref, down_row), (up_ref, up_row)):
                add_picked(
                    picks_ref, g_ref.shape[0], (adapters, lambda adapter, out_ref=out_ref: out_ref.at[0, 0, adapter]),
                    lambda at, row=row: g_ref[at, pl.ds(row, RANK), :],
                )


def proj_total(picks, gathered, projs, so_far, shape):
    first = projs[0]
    block = pl.BlockSpec((1, 1, *shape[2:]), lambda p, s: (0, p + first, 0, 0, 0))
    rest = [] if so_far is None else list(so_far)
    first_source = min(PROJ_ROWS[proj][0] for proj in projs)
    return pl.pallas_call(
        functools.partial(proj_total_kernel, tuple(projs), first_source, len(rest), len(gathered)),
        grid_spec=pltpu.PrefetchScalarGridSpec(
            num_scalar_prefetch=1,
            grid=(len(projs),),
            in_specs=[WHOLE] * len(gathered) + [ANY] * len(rest),
            out_specs=[block] * 2,
        ),
        out_shape=[jax.ShapeDtypeStruct(shape, F32)] * 2,
        input_output_aliases={1 + len(gathered) + at: at for at in range(len(rest))},
        name=f"proj_total_{first}",
        compiler_params=params(60),
        cost_estimate=cost(1.4 * len(projs)),
    )(picks, *gathered, *rest)


class Gathering:
    def __init__(self, shard, parts, across, sibling, together):
        self.shard, self.parts, self.across, self.sibling, self.together = shard, parts, across, sibling, together
        self.half = shard.shape[0] // 2

    def begin(self):
        self.x, self.y = self.across(self.shard, 1), self.across(self.shard, 2)
        self.own = self.sibling(self.shard)

    def forward(self):
        self.xy, self.yx = self.across(self.x[: self.half], 2), self.across(self.y[self.half :], 1)
        if self.together:
            self.near = [self.sibling(jnp.concatenate([self.x, self.y], axis=0))]
        else:
            self.near = [self.sibling(self.x), self.sibling(self.y)]

    def share(self):
        self.far = self.sibling(jnp.concatenate([self.xy, self.yx], axis=0))

    def result(self):
        rows, half = self.shard.shape[0], self.half
        arrays = [self.shard, self.own, self.x, self.y, *self.near, self.xy, self.yx, self.far]
        layout = [[(0, True, who, 0, rows)] for who in (0, 1, 2, 4)]
        if self.together:
            layout += [[(0, True, 3, 0, rows), (rows, True, 5, 0, rows)]]
        else:
            layout += [[(0, True, 3, 0, rows)], [(0, True, 5, 0, rows)]]
        layout += [[(0, True, 6, 0, half)], [(0, True, 6, half, rows - half)]]
        layout += [[(0, True, 7, 0, half), (half, True, 7, half, rows - half)]]
        return Gathered(arrays, layout, rows // self.parts)


class Whole:
    def __init__(self, shard, parts, shards, gather):
        self.shard, self.parts, self.shards, self.gather = shard, parts, shards, gather
        self.x = self.y = self.own = self.xy = self.yx = shard
        self.near = []

    def begin(self):
        self.whole = self.gather(self.shard)

    def forward(self):
        pass

    def share(self):
        pass

    def result(self):
        rows = self.shard.shape[0]
        return Gathered([self.whole], [[(at * rows, False, at, 0, rows) for at in range(self.shards)]], rows // self.parts)


def make_shards(mesh):
    chips, span = mesh.shape["chip"], mesh.shape["sp"]
    plane = ("chip", "core")

    def tie(*values):
        return lax.optimization_barrier(values)

    def turn(values, by):
        return lax.ppermute(values, "sp", [(i, (i + by) % span) for i in range(span)])

    def swap(values, bit):
        return lax.ppermute(values, "sp", [(i, i ^ bit) for i in range(span)])

    def across(values, bit):
        return lax.ppermute(values, "chip", [(i, i ^ bit) for i in range(chips)])

    def sibling(values):
        return lax.ppermute(values, "core", [(0, 1), (1, 0)])

    def gathering(shard, parts, steps, together=False):
        if chips == 4 and steps:
            return Gathering(shard, parts, across, sibling, together)
        return Whole(shard, parts, 2 * chips, lambda v: lax.all_gather(v, plane, axis=0, tiled=True))

    def shards(
        inputs,
        segments,
        enc_states,
        adapter_pick,
        qkv_weights,
        out_weights,
        mlp_in,
        mlp_out,
        proj_down,
        proj_up,
        fc1_down,
        fc1_up,
        fc2_down,
        fc2_up,
        cotangent,
    ):
        x_low = inputs[0]
        memory = enc_states[0]
        tokens, width = x_low.shape
        mem_rows = memory.shape[0]
        own = lax.axis_index("chip") * 2 + lax.axis_index("core")
        scalars = jnp.stack([lax.axis_index("sp"), own, adapter_pick[0]]).astype(jnp.int32)
        tables = (proj_down, proj_up)

        a = gathering(qkv_weights[0, :3].reshape(-1, width), 3, True)
        b_shard = jnp.concatenate([out_weights[0].reshape(-1, width), qkv_weights[0, 3:].reshape(-1, width)], axis=0)
        b = gathering(b_shard, 5, True, True)
        c, d = gathering(mlp_in[0], 1, False), gathering(mlp_out[0], 1, True, True)

        seg_row = jnp.pad(segments.astype(BF16), ((0, 15), (0, width - tokens)))
        ext = [jnp.concatenate([x_low, seg_row], axis=0)]
        lane = jnp.arange(AUG, dtype=jnp.int32)
        kinds = (lane >= TERMS) & (lane < TERMS + SEG_KINDS)
        q_seg = (kinds[:, None] & (lane[:, None] - TERMS == segments)).astype(F32)
        free_seg = jnp.zeros((AUG, tokens), F32)

        def key_aug(block):
            seg = block[tokens, :tokens].astype(jnp.int32)
            return jnp.where(lane[None] < TERMS, 1.0, jnp.where(kinds[None] & (lane[None] - TERMS != seg[:, None]), FAR, 0.0)).astype(BF16)

        free_aug = jnp.broadcast_to((lane[None] < TERMS).astype(BF16), (span * mem_rows, AUG))

        a.begin()
        ext.append(turn(ext[0], 1))
        a.x, a.y, a.own, ext[1] = tie(a.x, a.y, a.own, ext[1])
        a.forward()
        ext.append(turn(ext[1], 1))
        a.xy, a.yx, b.shard, ext[2], *a.near = tie(a.xy, a.yx, b.shard, ext[2], *a.near)
        a.share()
        b.begin()
        while len(ext) < span:
            ext.append(turn(ext[-1], 1))
        w_a = a.result()

        state, ks, vs, rs, augs = None, [], [], [], []
        q = o = None
        for at in range(0, span, 2):
            step = Step(f"self_{at}", w_a, (0, 1, 2) if at == 0 else (1, 2), (at, at + 1), at == 0, at == span - 2, True)
            if at:
                ext[at], ext[at + 1], state[1] = tie(ext[at], ext[at + 1], state[1])
            augs += [key_aug(ext[at]), key_aug(ext[at + 1])]
            q, k, v, r, out = attend_step(step, scalars, [[ext[at]], [ext[at + 1]]], tokens, tokens, tables, augs[at:], q, q_seg, state)
            ks, vs, rs = ks + k, vs + v, rs + r
            if at < span - 2:
                state = out if at == 0 else [state[0], *out]
            else:
                o, qa = out
            if at == 0:
                state[1], b.x, b.y, b.own, ext[-1], on, c.shard = tie(state[1], b.x, b.y, b.own, ext[-1], memory, c.shard)
                b.forward()
                c.begin()
                mems = [memory, turn(on, 1), *[None] * (span - 3), turn(on, -1)]
        o, mems[1], mems[-1], b.xy, b.yx, *b.near = tie(o, mems[1], mems[-1], b.xy, b.yx, *b.near)
        b.share()
        for by in range(2, span - 1):
            mems[by] = turn(mems[by - 1], 1)
        w_b = b.result()
        h1, h1_low, std1, r_mid, qc = mid("mid", scalars, o, x_low, 0, 6, True, *tables, w_b)
        qc, d.shard, *mems[1:] = tie(qc, d.shard, *mems[1:])
        d.begin()
        step = Step("cross", w_b, (3, 4), (0,), True, True, False)
        _, (kc,), (vc,), (r_mem,), (oc, qca) = attend_step(step, scalars, [mems], tokens, mem_rows, tables, [free_aug], qc, free_seg, None)
        oc, d.x, d.y, d.own = tie(oc, d.x, d.y, d.own)
        d.forward()
        h2, h2_low, std2, r_co = mid("mid_cross", scalars, oc, h1, 1, 7, False, *tables, w_b)
        w_c = c.result()
        g, slope, r_fc1 = gelu_up(scalars, h2_low, fc1_down, fc1_up, w_c)
        g, d.xy, d.yx, *d.near = tie(g, d.xy, d.yx, *d.near)
        d.share()
        w_d = d.result()
        y, d2, doc, gac, fc_grads = mlp(
            scalars, g, slope, h2, h2_low, std2, cotangent[0], r_fc1, r_co, oc,
            fc1_down, fc1_up, fc2_down, fc2_up, *tables, w_c, w_d, w_b,
        )
        g0 = lax.psum(fc_grads, "sp")

        step = Step("cross_back", w_b, (3, 4), (0,), True, True, False)
        dmem, parts, dqc, cross_grads = back_step(step, scalars, qca, gac, qc, doc, kc, vc, free_aug, r_mem, mems, mem_rows, tables, None, None)

        def mem_part(slot):
            return parts[(slot - 1) * mem_rows : slot * mem_rows]

        def added(slot, arrived):
            return (mem_part(slot).astype(F32) + arrived.astype(F32)).astype(BF16)

        middle = span // 2
        lower, upper = turn(mem_part(middle), -1), turn(mem_part(middle + 1), 1)
        d1, do, ga, mid_grads = mid_back(scalars, dqc, d2, h1, h1_low, std1, r_mid, o, *tables, w_b)
        g0, g1 = tie(g0, jnp.concatenate([mid_grads, cross_grads], axis=0))
        g1 = lax.psum(g1, "sp")
        g0 = g0[None]

        def doubled(values, bit):
            return jnp.concatenate([values, across(values, bit)], axis=0)

        bits = [1 << at for at in range(chips.bit_length() - 1)]
        state, moving, at_bit = None, None, 0
        for at in reversed(range(span)):
            step = Step(f"self_back_{at}", w_a, (0, 1, 2) if at == 0 else (1, 2), (at,), at == span - 1, at == 0, True)
            out = back_step(step, scalars, qa, ga, q, do, ks[at], vs[at], augs[at], rs[at], [ext[at]], tokens, tables, state, d1)
            if at == 0:
                dx, g2 = out
                dx, g2, moving, g0, g1 = tie(dx, g2, moving, g0, g1)
                dx = dx + moving.astype(F32)
            else:
                part, *state = out
                if at == span - 1:
                    part, state[0], lower, upper = tie(part, state[0], lower, upper)
                    for slot in range(middle - 1, 1, -1):
                        lower = turn(added(slot, lower), -1)
                    for slot in range(middle + 2, span):
                        upper = turn(added(slot, upper), 1)
                    lower = added(1, lower)
                else:
                    part, state[0], moving, g0, *on = tie(part, state[0], moving, g0, *([g1] if at == 1 else []))
                    part = (part.astype(F32) + moving.astype(F32)).astype(BF16)
                    part, state[0] = tie(part, state[0])
                moving = turn(part, -1)
                if at_bit < len(bits):
                    g0 = doubled(g0, bits[at_bit])
                    at_bit += 1
                if at == 1:
                    while at_bit < len(bits):
                        g0 = doubled(g0, bits[at_bit])
                        at_bit += 1
                    g1 = doubled(on[0][None], bits[0])
        g0 = jnp.concatenate([g0, sibling(g0)], axis=0)
        g2 = (g2.astype(F32) + swap(g2, 1).astype(F32)).astype(BF16)
        g2, g1, g0 = tie(g2, g1, g0)
        for bit in bits[1:]:
            g1 = doubled(g1, bit)
        picks = g0[:, FC_ROWS["pick"], 0].astype(jnp.int32)
        fcs = fc_total(picks, g0, (fc1_down.shape, fc1_up.shape, fc2_down.shape, fc2_up.shape))
        bit = 2
        while bit < span:
            g2 = (g2.astype(F32) + swap(g2, bit).astype(F32)).astype(BF16)
            bit *= 2
        g2, g1, lower, picks, *fcs = tie(g2, g1, lower, picks, *fcs)
        lower = turn(lower, -1)
        g1 = jnp.concatenate([g1, sibling(g1)], axis=0)
        g2 = doubled(g2[None], bits[0])
        g2, g1, picks = tie(g2, g1, picks)
        projs = proj_total(picks, (g0, g1), range(3, 8), None, proj_down.shape)
        for bit in bits[1:]:
            g2 = doubled(g2, bit)
        g2, *projs = tie(g2, *projs)
        g2 = jnp.concatenate([g2, sibling(g2)], axis=0)
        projs = proj_total(picks, (g2,), range(3), projs, proj_down.shape)
        dmem = dmem + lower.astype(F32) + upper.astype(F32)
        return (y[None], dx[None], dmem[None], *projs, *fcs)

    return shards


def solution(mesh):
    count = mesh.shape["fsdp"]
    fine = Mesh(mesh.devices.reshape(count // 2, 2, mesh.shape["sp"]), ("chip", "core", "sp"))
    fsdp = ("chip", "core")
    row = P(fsdp, "sp", None)
    return jax.shard_map(
        make_shards(fine),
        mesh=fine,
        in_specs=(
            row,
            P(fsdp, "sp"),
            row,
            P(fsdp),
            P(None, None, fsdp, None),
            P(None, None, fsdp, None),
            P(None, fsdp, None),
            P(None, fsdp, None),
            P(),
            P(),
            P(),
            P(),
            P(),
            P(),
            row,
        ),
        out_specs=(row, row, row, P(), P(), P(), P(), P(), P()),
        check_vma=False,
    )
```

profile of v0, /device:TPU:0, one launch (start us, length us, event | category | flops | bytes accessed | tf_op | source)
XLA Modules:
  0.0 432.6 jit_solution(15687862152573249708)
XLA Ops:
  15.7 17.0 %collective-permute-done.1.refs_10_.refs_12_.refs_14_.refs_16_.refs_17_ = bf16[384,1024]{1,0:T(8,128)(2,1)} collective-permute-done((bf16[384,1024]{1,0:T(8,128)(2,1)S(1)}, bf16[384,1024]{1,0:T(8,128)(2,1)}, u32[]{:S(2)}, u32[]{:S(2)}) %collective-permute-start.1) | collective-permute-done | bytes 786464 | tf_op jit(solution)/shard_map/ppermute | solution.py:1061
  42.0 7.2 %collective-permute-done.5.refs_14_.refs_16_.refs_18_.refs_20_.refs_21_ = bf16[192,1024]{1,0:T(8,128)(2,1)S(1)} collective-permute-done((bf16[192,1024]{1,0:T(8,128)(2,1)S(1)}, bf16[192,1024]{1,0:T(8,128)(2,1)S(1)}, u32[]{:S(2)}, u32[]{:S(2)}) %collective-permute-start.5) | collective-permute-done | bytes 393248 | tf_op jit(solution)/shard_map/ppermute | solution.py:1061
  62.0 13.9 %self_0.1 = (bf16[384,1024]{1,0:T(8,128)(2,1)}, bf16[384,1024]{1,0:T(8,128)(2,1)}, bf16[384,1024]{1,0:T(8,128)(2,1)}, bf16[384,1024]{1,0:T(8,128)(2,1)}, bf16[38...) custom-call(s32[3]{0:T(128)} %pad_add_fusion.sc_ref, ...), custom_call_target="tpu_custom_call" | custom-call | flops 27599998976 | tf_op jit(solution)/shard_map/self_0/pallas_call | solution.py:404
  75.9 6.9 %collective-permute-done.13.refs_1_.refs_10_ = bf16[400,1024]{1,0:T(8,128)(2,1)} collective-permute-done((bf16[400,1024]{1,0:T(8,128)(2,1)}, bf16[400,1024]{1,0:T(8,128)(2,1)}, u32[]{:S(2)}, u32[]{:S(2)}) %collective-permute-start.13) | collective-permute-done | bytes 819232 | tf_op jit(solution)/shard_map/ppermute | solution.py:1055
  82.8 7.1 %collective-permute-done.11.refs_3_.refs_12_.refs_17_ = bf16[640,1024]{1,0:T(8,128)(2,1)S(1)} collective-permute-done((bf16[640,1024]{1,0:T(8,128)(2,1)}, bf16[640,1024]{1,0:T(8,128)(2,1)S(1)}, u32[]{:S(2)}, u32[]{:S(2)}) %collective-permute-start.11) | collective-permute-done | bytes 1310752 | tf_op jit(solution)/shard_map/ppermute | solution.py:1061
  100.5 7.1 %self_2.1 = (bf16[384,1024]{1,0:T(8,128)(2,1)}, bf16[384,1024]{1,0:T(8,128)(2,1)}, bf16[384,1024]{1,0:T(8,128)(2,1)}, bf16[384,1024]{1,0:T(8,128)(2,1)}, bf16[38...) custom-call(s32[3]{0:T(128)} %pad_add_fusion.sc_ref, ...), custom_call_target="tpu_custom_call" | custom-call | flops 27599998976 | tf_op jit(solution)/shard_map/self_2/pallas_call | solution.py:404
  107.6 7.2 %collective-permute-done.14.refs_1_.refs_11_ = bf16[256,1024]{1,0:T(8,128)(2,1)} collective-permute-done((bf16[256,1024]{1,0:T(8,128)(2,1)}, bf16[256,1024]{1,0:T(8,128)(2,1)}, u32[]{:S(2)}, u32[]{:S(2)}) %collective-permute-start.14) | collective-permute-done | bytes 524320 | tf_op jit(solution)/shard_map/ppermute | solution.py:1055
  114.8 5.9 %collective-permute-done.17.refs_6_.refs_15_.refs_20_ = bf16[320,1024]{1,0:T(8,128)(2,1)S(1)} collective-permute-done((bf16[320,1024]{1,0:T(8,128)(2,1)}, bf16[320,1024]{1,0:T(8,128)(2,1)S(1)}, u32[]{:S(2)}, u32[]{:S(2)}) %collective-permute-start.17) | collective-permute-done | bytes 655392 | tf_op jit(solution)/shard_map/ppermute | solution.py:1061
  126.9 8.2 %mid.1 = (f32[384,1024]{1,0:T(8,128)}, bf16[384,1024]{1,0:T(8,128)(2,1)}, f32[384,1]{1,0:T(8,128)}, bf16[384,32]{1,0:T(8,128)(2,1)}, bf16[384,1024]{1,0:T(8,128)(2,1)}) custom-call(s32[3]{0:T(128)} %pad_add_fusion.sc_ref, bf16[384,1024]{1,0:T(8,128)(2,1)} %get-tuple-element.178.o_ref, bf16[384,1024]{1,0:T(8,128)(2,1)} %bitcast.19, ...), custom_call_target="tpu_custom_call" | custom-call | flops 1150000000 | tf_op jit(solution)/shard_map/mid/pallas_call | solution.py:654
  135.1 6.2 %collective-permute-done.20.refs_2_.refs_12_ = bf16[256,1024]{1,0:T(8,128)(2,1)S(1)} collective-permute-done((bf16[256,1024]{1,0:T(8,128)(2,1)}, bf16[256,1024]{1,0:T(8,128)(2,1)S(1)}, u32[]{:S(2)}, u32[]{:S(2)}) %collective-permute-start.20) | collective-permute-done | bytes 524320 | tf_op jit(solution)/shard_map/ppermute | solution.py:1055
  144.5 23.7 %cross.1 = (bf16[1024,1024]{1,0:T(8,128)(2,1)}, bf16[1024,1024]{1,0:T(8,128)(2,1)}, bf16[1024,32]{1,0:T(8,128)(2,1)}, bf16[384,1024]{1,0:T(8,128)(2,1)}, bf16[8,144,768]{2,1,0:T(8,128)(2,1)}) custom-call(s32[3]{0:T(128)} %pad_add_fusion.sc_ref, bf16[256,1024]{1,0:T(8,128)(2,1)} %bitcast.45, bf16[256,1024]{1,0:T(8,128)(2,1)} %collective-permute-done.14.refs_1_.refs_11_, ...), custom_call_target="tpu_custom_call" | custom-call | flops 36800000000 | tf_op jit(solution)/shard_map/cross/pallas_call | solution.py:404
  176.7 7.3 %mid_cross.1 = (f32[384,1024]{1,0:T(8,128)}, bf16[384,1024]{1,0:T(8,128)(2,1)}, f32[384,1]{1,0:T(8,128)}, bf16[384,16]{1,0:T(8,128)(2,1)}) custom-call(s32[3]{0:T(128)} %pad_add_fusion.sc_ref, bf16[384,1024]{1,0:T(8,128)(2,1)} %get-tuple-element.192.o_ref.oc_ref, f32[384,1024]{1,0:T(8,128)} %get-tuple-element.193.x_ref.h1_ref, ...), custom_call_target="tpu_custom_call" | custom-call | flops 1150000000 | tf_op jit(solution)/shard_map/mid_cross/pallas_call | solution.py:654
  184.0 15.4 %gelu_up.1 = (bf16[384,4096]{1,0:T(8,128)(2,1)}, bf16[384,4096]{1,0:T(8,128)(2,1)}, bf16[384,16]{1,0:T(8,128)(2,1)}) custom-call(s32[3]{0:T(128)} %pad_add_fusion.sc_ref, bf16[384,1024]{1,0:T(8,128)(2,1)} %get-tuple-element.194.x_ref.h2_low_ref, bf16[1,8,16,1024]{3,2,1,0:T(8,128)(2,1)} %a1_ref.1, bf16[1,8,16,4096]{3,2,1,0:T(8,128)(2,1)} %b1_ref.1, ...), custom_call_target="tpu_custom_call" | custom-call | flops 17250000896 | tf_op jit(solution)/shard_map/gelu_up/pallas_call | solution.py:691
  203.3 33.2 %mlp.1 = (bf16[384,1024]{1,0:T(8,128)(2,1)}, f32[384,1024]{1,0:T(8,128)}, bf16[384,1024]{1,0:T(8,128)(2,1)}, bf16[8,144,768]{2,1,0:T(8,128)(2,1)}, bf16[208,1024]{1,0:T(8,128)(2,1)}) custom-call(s32[3]{0:T(128)} %pad_add_fusion.sc_ref, bf16[384,4096]{1,0:T(8,128)(2,1)} %get-tuple-element.199.g_ref, bf16[384,4096]{1,0:T(8,128)(2,1)} %get-tuple-element.200.slope_ref, ...), custom_call_target="tpu_custom_call" | custom-call | flops 37950001152 | tf_op jit(solution)/shard_map/mlp/pallas_call | solution.py:802
  236.8 28.3 %cross_back.1 = (f32[256,1024]{1,0:T(8,128)}, bf16[768,1024]{1,0:T(8,128)(2,1)}, bf16[384,1024]{1,0:T(8,128)(2,1)}, bf16[64,1024]{1,0:T(8,128)(2,1)}) custom-call(s32[3]{0:T(128)} %pad_add_fusion.sc_ref, bf16[8,144,768]{2,1,0:T(8,128)(2,1)} %get-tuple-element.211.refs_0_, bf16[8,144,768]{2,1,0:T(8,128)(2,1)} %get-tuple-element.212.refs_1_, ...), custom_call_target="tpu_custom_call" | custom-call | flops 49066668032 | tf_op jit(solution)/shard_map/cross_back/pallas_call | solution.py:581
  270.4 10.5 %mid_back.1 = (f32[384,1024]{1,0:T(8,128)}, bf16[384,1024]{1,0:T(8,128)(2,1)}, bf16[8,144,768]{2,1,0:T(8,128)(2,1)}, bf16[64,1024]{1,0:T(8,128)(2,1)}) custom-call(s32[3]{0:T(128)} %pad_add_fusion.sc_ref, bf16[384,1024]{1,0:T(8,128)(2,1)} %get-tuple-element.217.dqc_ref, f32[384,1024]{1,0:T(8,128)} %get-tuple-element.218.d2_ref, ...), custom_call_target="tpu_custom_call" | custom-call | flops 1150000000 | tf_op jit(solution)/shard_map/mid_back/pallas_call | solution.py:888
  281.0 6.4 %self_back_3.1 = (bf16[384,1024]{1,0:T(8,128)(2,1)}, f32[8,128,384]{2,1,0:T(8,128)}, f32[64,1024]{1,0:T(8,128)}) custom-call(s32[3]{0:T(128)} %pad_add_fusion.sc_ref, bf16[8,144,768]{2,1,0:T(8,128)(2,1)} %get-tuple-element.210.refs_0_, bf16[8,144,768]{2,1,0:T(8,128)(2,1)} %get-tuple-element.222.refs_1_, bf16[384,1024]{1,0:T(8,128)(2,1)} %get-tuple-element.223.refs_2_, ...), custom_call_target="tpu_custom_call" | custom-call | flops 18400000000 | tf_op jit(solution)/shard_map/self_back_3/pallas_call | solution.py:581
  299.7 6.8 %self_back_2.1 = (bf16[384,1024]{1,0:T(8,128)(2,1)}, f32[8,128,384]{2,1,0:T(8,128)}, f32[64,1024]{1,0:T(8,128)}) custom-call(s32[3]{0:T(128)} %pad_add_fusion.sc_ref, bf16[8,144,768]{2,1,0:T(8,128)(2,1)} %get-tuple-element.210.refs_0_, bf16[8,144,768]{2,1,0:T(8,128)(2,1)} %get-tuple-element.222.refs_1_, bf16[384,1024]{1,0:T(8,128)(2,1)} %get-tuple-element.223.refs_2_, ...), custom_call_target="tpu_custom_call" | custom-call | flops 18400000000 | tf_op jit(solution)/shard_map/self_back_2/pallas_call | solution.py:581
  306.7 13.8 %collective-permute-done.30 = bf16[384,1024]{1,0:T(8,128)(2,1)S(1)} collective-permute-done((bf16[384,1024]{1,0:T(8,128)(2,1)}, bf16[384,1024]{1,0:T(8,128)(2,1)S(1)}, u32[]{:S(2)}, u32[]{:S(2)}) %collective-permute-start.30) | collective-permute-done | bytes 786464 | tf_op jit(solution)/shard_map/ppermute | solution.py:1055
  326.7 6.7 %self_back_1.1 = (bf16[384,1024]{1,0:T(8,128)(2,1)}, f32[8,128,384]{2,1,0:T(8,128)}, f32[64,1024]{1,0:T(8,128)}) custom-call(s32[3]{0:T(128)} %pad_add_fusion.sc_ref, bf16[8,144,768]{2,1,0:T(8,128)(2,1)} %get-tuple-element.210.refs_0_, bf16[8,144,768]{2,1,0:T(8,128)(2,1)} %get-tuple-element.222.refs_1_, bf16[384,1024]{1,0:T(8,128)(2,1)} %get-tuple-element.223.refs_2_, ...), custom_call_target="tpu_custom_call" | custom-call | flops 18400000000 | tf_op jit(solution)/shard_map/self_back_1/pallas_call | solution.py:581
  333.4 12.5 %collective-permute-done.33 = bf16[2,208,1024]{2,1,0:T(8,128)(2,1)S(1)} collective-permute-done((bf16[2,208,1024]{2,1,0:T(8,128)(2,1)S(1)}, bf16[2,208,1024]{2,1,0:T(8,128)(2,1)S(1)}, u32[]{:S(2)}, u32[]{:S(2)}) %collective-permute-start.33) | collective-permute-done | bytes 852000 | tf_op jit(solution)/shard_map/ppermute | solution.py:1061
  353.6 16.2 %self_back_0.1 = (f32[384,1024]{1,0:T(8,128)}, bf16[96,1024]{1,0:T(8,128)(2,1)}) custom-call(s32[3]{0:T(128)} %pad_add_fusion.sc_ref, bf16[8,144,768]{2,1,0:T(8,128)(2,1)} %get-tuple-element.210.refs_0_, bf16[8,144,768]{2,1,0:T(8,128)(2,1)} %get-tuple-element.222.refs_1_, bf16[384,1024]{1,0:T(8,128)(2,1)} %get-tuple-element.223.refs_2_, ...), custom_call_target="tpu_custom_call" | custom-call | flops 18400000000 | tf_op jit(solution)/shard_map/self_back_0/pallas_call | solution.py:581
  372.4 6.1 %collective-permute-done.36 = bf16[96,1024]{1,0:T(8,128)(2,1)S(1)} collective-permute-done((bf16[96,1024]{1,0:T(8,128)(2,1)}, bf16[96,1024]{1,0:T(8,128)(2,1)S(1)}, u32[]{:S(2)}, u32[]{:S(2)}) %collective-permute-start.36) | collective-permute-done | bytes 196640 | tf_op jit(solution)/shard_map/ppermute | solution.py:1058
  407.0 6.7 %proj_total_3.1 = (f32[1,8,8,16,1024]{4,3,2,1,0:T(8,128)}, f32[1,8,8,16,1024]{4,3,2,1,0:T(8,128)}) custom-call(s32[8]{0:T(128)} %convert_reduce_fusion.picks_ref, bf16[8,208,1024]{2,1,0:T(8,128)(2,1)} %copy-done.4, bf16[8,128,1024]{2,1,0:T(8,128)(2,1)} %pad_maximum_fusion.3.refs_1_), custom_call_target="tpu_custom_call" | custom-call | flops 8049999872 | tf_op jit(solution)/shard_map/proj_total_3/pallas_call | solution.py:979
  (197 shorter events, 137.5 us)
Async XLA Ops:
  7.2 176.8 %all-gather.2.cloned.1.call-start = ((), (), s32[]{:S(2)}) async-start(), calls=%async_computation | async-start | bytes 9437184 | tf_op jit(solution)/shard_map/all_gather | solution.py:1069
  9.3 24.6 %collective-permute-start.3 = (bf16[400,1024]{1,0:T(8,128)(2,1)S(1)}, bf16[400,1024]{1,0:T(8,128)(2,1)}, u32[]{:S(2)}, u32[]{:S(2)}) collective-permute-start(bf16[400,1024]{1,0:T(8,128)(2,1)S(1)} %fusion.1.refs_0_.refs_10_), channel_id=1, source_target_pairs={{0,1},{1,2},{2,3},{3,0},{4,5},{5,6},{6,7},{7,4},{8,9},{9,10},{10,1... | collective-permute-start | bytes 2457608 | tf_op jit(solution)/shard_map/ppermute | solution.py:1055
  33.9 21.6 %collective-permute-start.6 = (bf16[400,1024]{1,0:T(8,128)(2,1)}, bf16[400,1024]{1,0:T(8,128)(2,1)}, u32[]{:S(2)}, u32[]{:S(2)}) collective-permute-start(bf16[400,1024]{1,0:T(8,128)(2,1)} %collective-permute-done.3.refs_1_.refs_10_), channel_id=1, source_target_pairs={{0,1},{1,2},{2,3},{3,0},{4,5},{5,6},{6,7},{7,4},{8,9},{9,10},{10,1... | collective-permute-start | bytes 2457608 | tf_op jit(solution)/shard_map/ppermute | solution.py:1055
  58.5 24.3 %collective-permute-start.12 = (bf16[640,1024]{1,0:T(8,128)(2,1)}, bf16[640,1024]{1,0:T(8,128)(2,1)}, u32[]{:S(2)}, u32[]{:S(2)}) collective-permute-start(bf16[640,1024]{1,0:T(8,128)(2,1)} %pad_maximum_fusion.6.refs_0_.refs_9_.refs_14_), channel_id=1, source_target_pairs={{0,4},{4,0},{1,5},{5,1},{2,6},{6,2},{3,7},{7,3},{8,12},{12,8},{9,1... | collective-permute-start | bytes 3932168 | tf_op jit(solution)/shard_map/ppermute | solution.py:1064
  59.0 30.9 %collective-permute-start.11 = (bf16[640,1024]{1,0:T(8,128)(2,1)}, bf16[640,1024]{1,0:T(8,128)(2,1)S(1)}, u32[]{:S(2)}, u32[]{:S(2)}) collective-permute-start(bf16[640,1024]{1,0:T(8,128)(2,1)} %pad_maximum_fusion.6.refs_0_.refs_9_.refs_14_), channel_id=1, source_target_pairs={{0,16},{8,24},{16,0},{24,8},{1,17},{9,25},{17,1},{25,9},{2,18},{10... | collective-permute-start | bytes 3932168 | tf_op jit(solution)/shard_map/ppermute | solution.py:1061
  59.6 30.6 %collective-permute-start.10 = (bf16[640,1024]{1,0:T(8,128)(2,1)}, bf16[640,1024]{1,0:T(8,128)(2,1)S(1)}, u32[]{:S(2)}, u32[]{:S(2)}) collective-permute-start(bf16[640,1024]{1,0:T(8,128)(2,1)} %pad_maximum_fusion.6.refs_0_.refs_9_.refs_14_), channel_id=1, source_target_pairs={{0,8},{8,0},{16,24},{24,16},{1,9},{9,1},{17,25},{25,17},{2,10},{10... | collective-permute-start | bytes 3932168 | tf_op jit(solution)/shard_map/ppermute | solution.py:1061
  61.1 21.7 %collective-permute-start.13 = (bf16[400,1024]{1,0:T(8,128)(2,1)}, bf16[400,1024]{1,0:T(8,128)(2,1)}, u32[]{:S(2)}, u32[]{:S(2)}) collective-permute-start(bf16[400,1024]{1,0:T(8,128)(2,1)} %collective-permute-done.6.refs_0_.refs_10_), channel_id=1, source_target_pairs={{0,1},{1,2},{2,3},{3,0},{4,5},{5,6},{6,7},{7,4},{8,9},{9,10},{10,1... | collective-permute-start | bytes 2457608 | tf_op jit(solution)/shard_map/ppermute | solution.py:1055
  90.3 197.8 %all-reduce.4.cloned.1.call-start = ((), (), s32[]{:S(2)}) async-start(), calls=%async_computation.1 | async-start | bytes 851968 | tf_op jit(solution)/shard_map/psum | solution.py:1166
  90.9 24.0 %collective-permute-start.14 = (bf16[256,1024]{1,0:T(8,128)(2,1)}, bf16[256,1024]{1,0:T(8,128)(2,1)}, u32[]{:S(2)}, u32[]{:S(2)}) collective-permute-start(bf16[256,1024]{1,0:T(8,128)(2,1)} %bitcast.44), channel_id=1, source_target_pairs={{0,1},{1,2},{2,3},{3,0},{4,5},{5,6},{6,7},{7,4},{8,9},{9,10},{10,1... | collective-permute-start | bytes 1572872 | tf_op jit(solution)/shard_map/ppermute | solution.py:1055
  94.3 26.4 %collective-permute-start.17 = (bf16[320,1024]{1,0:T(8,128)(2,1)}, bf16[320,1024]{1,0:T(8,128)(2,1)S(1)}, u32[]{:S(2)}, u32[]{:S(2)}) collective-permute-start(bf16[320,1024]{1,0:T(8,128)(2,1)} %slice.54), channel_id=1, source_target_pairs={{0,8},{8,0},{16,24},{24,16},{1,9},{9,1},{17,25},{25,17},{2,10},{10... | collective-permute-start | bytes 1966088 | tf_op jit(solution)/shard_map/ppermute | solution.py:1061
  95.8 26.2 %collective-permute-start.16 = (bf16[320,1024]{1,0:T(8,128)(2,1)}, bf16[320,1024]{1,0:T(8,128)(2,1)}, u32[]{:S(2)}, u32[]{:S(2)}) collective-permute-start(bf16[320,1024]{1,0:T(8,128)(2,1)} %slice.53), channel_id=1, source_target_pairs={{0,16},{8,24},{16,0},{24,8},{1,17},{9,25},{17,1},{25,9},{2,18},{10... | collective-permute-start | bytes 1966088 | tf_op jit(solution)/shard_map/ppermute | solution.py:1061
  99.0 23.1 %collective-permute-start.18 = (bf16[1280,1024]{1,0:T(8,128)(2,1)}, bf16[1280,1024]{1,0:T(8,128)(2,1)S(1)}, u32[]{:S(2)}, u32[]{:S(2)}) collective-permute-start(bf16[1280,1024]{1,0:T(8,128)(2,1)} %pad_maximum_fusion.1), channel_id=1, source_target_pairs={{0,4},{4,0},{1,5},{5,1},{2,6},{6,2},{3,7},{7,3},{8,12},{12,8},{9,1... | collective-permute-start | bytes 7864328 | tf_op jit(solution)/shard_map/ppermute | solution.py:1064
  142.1 26.2 %collective-permute-start.23 = (bf16[512,1024]{1,0:T(8,128)(2,1)}, bf16[512,1024]{1,0:T(8,128)(2,1)S(1)}, u32[]{:S(2)}, u32[]{:S(2)}) collective-permute-start(bf16[512,1024]{1,0:T(8,128)(2,1)} %bitcast.38), channel_id=1, source_target_pairs={{0,4},{4,0},{1,5},{5,1},{2,6},{6,2},{3,7},{7,3},{8,12},{12,8},{9,1... | collective-permute-start | bytes 3145736 | tf_op jit(solution)/shard_map/ppermute | solution.py:1064
  142.1 30.6 %collective-permute-start.22 = (bf16[512,1024]{1,0:T(8,128)(2,1)}, bf16[512,1024]{1,0:T(8,128)(2,1)S(1)}, u32[]{:S(2)}, u32[]{:S(2)}) collective-permute-start(bf16[512,1024]{1,0:T(8,128)(2,1)} %bitcast.39), channel_id=1, source_target_pairs={{0,16},{8,24},{16,0},{24,8},{1,17},{9,25},{17,1},{25,9},{2,18},{10... | collective-permute-start | bytes 3145736 | tf_op jit(solution)/shard_map/ppermute | solution.py:1061
  142.7 30.0 %collective-permute-start.21 = (bf16[512,1024]{1,0:T(8,128)(2,1)}, bf16[512,1024]{1,0:T(8,128)(2,1)S(1)}, u32[]{:S(2)}, u32[]{:S(2)}) collective-permute-start(bf16[512,1024]{1,0:T(8,128)(2,1)} %bitcast.40), channel_id=1, source_target_pairs={{0,8},{8,0},{16,24},{24,16},{1,9},{9,1},{17,25},{25,17},{2,10},{10... | collective-permute-start | bytes 3145736 | tf_op jit(solution)/shard_map/ppermute | solution.py:1061
  174.3 25.2 %collective-permute-start.26 = (bf16[1024,1024]{1,0:T(8,128)(2,1)}, bf16[1024,1024]{1,0:T(8,128)(2,1)}, u32[]{:S(2)}, u32[]{:S(2)}) collective-permute-start(bf16[1024,1024]{1,0:T(8,128)(2,1)} %pad_maximum_fusion.2), channel_id=1, source_target_pairs={{0,4},{4,0},{1,5},{5,1},{2,6},{6,2},{3,7},{7,3},{8,12},{12,8},{9,1... | collective-permute-start | bytes 6291464 | tf_op jit(solution)/shard_map/ppermute | solution.py:1064
  174.6 24.8 %collective-permute-start.25 = (bf16[256,1024]{1,0:T(8,128)(2,1)S(1)}, bf16[256,1024]{1,0:T(8,128)(2,1)S(1)}, u32[]{:S(2)}, u32[]{:S(2)}) collective-permute-start(bf16[256,1024]{1,0:T(8,128)(2,1)S(1)} %slice.56), channel_id=1, source_target_pairs={{0,8},{8,0},{16,24},{24,16},{1,9},{9,1},{17,25},{25,17},{2,10},{10... | collective-permute-start | bytes 1572872 | tf_op jit(solution)/shard_map/ppermute | solution.py:1061
  176.2 23.3 %collective-permute-start.24 = (bf16[256,1024]{1,0:T(8,128)(2,1)S(1)}, bf16[256,1024]{1,0:T(8,128)(2,1)S(1)}, u32[]{:S(2)}, u32[]{:S(2)}) collective-permute-start(bf16[256,1024]{1,0:T(8,128)(2,1)S(1)} %slice.55), channel_id=1, source_target_pairs={{0,16},{8,24},{16,0},{24,8},{1,17},{9,25},{17,1},{25,9},{2,18},{10... | collective-permute-start | bytes 1572872 | tf_op jit(solution)/shard_map/ppermute | solution.py:1061
  236.6 109.5 %all-reduce.6.cloned.1.call-start = ((), (), s32[]{:S(2)}) async-start(), calls=%async_computation.2 | async-start | bytes 524288 | tf_op jit(solution)/shard_map/psum | solution.py:1181
  266.4 23.0 %collective-permute-start.29 = (bf16[256,1024]{1,0:T(8,128)(2,1)S(1)}, bf16[256,1024]{1,0:T(8,128)(2,1)S(1)}, u32[]{:S(2)}, u32[]{:S(2)}) collective-permute-start(bf16[256,1024]{1,0:T(8,128)(2,1)S(1)} %get-tuple-element.305), channel_id=1, source_target_pairs={{0,1},{1,2},{2,3},{3,0},{4,5},{5,6},{6,7},{7,4},{8,9},{9,10},{10,1... | collective-permute-start | bytes 1572872 | tf_op jit(solution)/shard_map/ppermute | solution.py:1055
  267.9 27.1 %collective-permute-start.28 = (bf16[256,1024]{1,0:T(8,128)(2,1)S(1)}, bf16[256,1024]{1,0:T(8,128)(2,1)}, u32[]{:S(2)}, u32[]{:S(2)}) collective-permute-start(bf16[256,1024]{1,0:T(8,128)(2,1)S(1)} %get-tuple-element.306), channel_id=1, source_target_pairs={{0,3},{1,0},{2,1},{3,2},{4,7},{5,4},{6,5},{7,6},{8,11},{9,8},{10,9... | collective-permute-start | bytes 1572872 | tf_op jit(solution)/shard_map/ppermute | solution.py:1055
  295.0 25.4 %collective-permute-start.30 = (bf16[384,1024]{1,0:T(8,128)(2,1)}, bf16[384,1024]{1,0:T(8,128)(2,1)S(1)}, u32[]{:S(2)}, u32[]{:S(2)}) collective-permute-start(bf16[384,1024]{1,0:T(8,128)(2,1)} %get-tuple-element.244), channel_id=1, source_target_pairs={{0,3},{1,0},{2,1},{3,2},{4,7},{5,4},{6,5},{7,6},{8,11},{9,8},{10,9... | collective-permute-start | bytes 2359304 | tf_op jit(solution)/shard_map/ppermute | solution.py:1055
  321.6 25.2 %collective-permute-start.32 = (bf16[384,1024]{1,0:T(8,128)(2,1)}, bf16[384,1024]{1,0:T(8,128)(2,1)}, u32[]{:S(2)}, u32[]{:S(2)}) collective-permute-start(bf16[384,1024]{1,0:T(8,128)(2,1)} %add_convert_fusion.1), channel_id=1, source_target_pairs={{0,3},{1,0},{2,1},{3,2},{4,7},{5,4},{6,5},{7,6},{8,11},{9,8},{10,9... | collective-permute-start | bytes 2359304 | tf_op jit(solution)/shard_map/ppermute | solution.py:1055
  349.1 21.8 %collective-permute-start.34 = (bf16[384,1024]{1,0:T(8,128)(2,1)S(1)}, bf16[384,1024]{1,0:T(8,128)(2,1)S(1)}, u32[]{:S(2)}, u32[]{:S(2)}) collective-permute-start(bf16[384,1024]{1,0:T(8,128)(2,1)S(1)} %add_convert_fusion), channel_id=1, source_target_pairs={{0,3},{1,0},{2,1},{3,2},{4,7},{5,4},{6,5},{7,6},{8,11},{9,8},{10,9... | collective-permute-start | bytes 2359304 | tf_op jit(solution)/shard_map/ppermute | solution.py:1055
  (54 other events, 522.7 us)
Sparse Core Ops, SparseCore 0:
  90.4 66.6 all-gather.1
  236.7 48.5 all-reduce.3
  288.2 54.7 all-reduce.5
where the time goes:
time: 440 us; the launch traced here: 433 us
  Pallas kernels  200 us (45%)
  waiting for transfers between devices  131 us (30%)
  starting transfers between devices  49.1 us (11%)
  other arithmetic  25.8 us (6%)
  between operations  15.2 us (3%)
  local copies, waits for them, and re-layouts  11.5 us (3%)
    ppermute x18, waiting for transfers between devices, across(): return lax.ppermute(values, 'chip', [(i, i ^ bit) for i in range(chips)])  70.3 us
    pallas_call x5, Pallas kernels, back_step(): pl.pallas_call(functools.partial(back_step_kernel, step, len(xs)), grid_s...  64.3 us
    ppermute x12, waiting for transfers between devices, turn(): lax.ppermute(values, 'sp', [(i, (i + by) % span) for i in range(span)])  45.4 us
    pallas_call x3, Pallas kernels, attend_step(): out = list(call(scalars, *args, *step.w.arrays))  44.7 us
    pallas_call x1, Pallas kernels, mlp(): pl.pallas_call(functools.partial(mlp_kernel, w_up, w_down, w_mid), grid_s...  33.2 us
    ppermute x12, starting transfers between devices, turn(): lax.ppermute(values, 'sp', [(i, (i + by) % span) for i in range(span)])  26.3 us
    ppermute x18, starting transfers between devices, across(): return lax.ppermute(values, 'chip', [(i, i ^ bit) for i in range(chips)])  18.2 us
    pallas_call x2, Pallas kernels, mid(): pl.pallas_call(functools.partial(mid_kernel, w, part, query), grid_spec=p...  15.5 us
  transfers between devices with their start and end apart: 48, of which 24 were waited for; matrix products, arithmetic and copies ran while one was open for 6% of the time, Pallas kernels for 38%

commit v1 on v0

--- a/solution.py
+++ b/solution.py
@@ -196,6 +196,14 @@
     def specs(self):
         return [ANY] * len(self.arrays)
 
+    def groups(self):
+        groups, at = {}, 0
+        for entries in self.layout:
+            for _, flip, who, _, _ in entries:
+                groups.setdefault((flip, who), []).append(at)
+                at += 1
+        return groups.items()
+
     def sems(self, parts):
         return pltpu.SemaphoreType.DMA((parts, self.count))
 
@@ -231,6 +239,22 @@
     return slice(pair * PAIR, (pair + 1) * PAIR)
 
 
+def key_rows(seg_ref, keys):
+    at = lax.broadcasted_iota(jnp.int32, (AUG, keys), 0)
+    if seg_ref is None:
+        return jnp.where(at < TERMS, 1.0, 0.0)
+    other = (at.astype(F32) - TERMS != seg_ref[0:1, :keys].astype(F32)) & (at < TERMS + SEG_KINDS)
+    return jnp.where(at < TERMS, 1.0, jnp.where(other, FAR, 0.0))
+
+
+def query_rows(seg_ref, queries):
+    at = lax.broadcasted_iota(jnp.int32, (AUG, queries), 0)
+    if seg_ref is None:
+        return jnp.zeros((AUG, queries), F32)
+    same = (at.astype(F32) - TERMS == seg_ref[0:1, :queries].astype(F32)) & (at >= TERMS) & (at < TERMS + SEG_KINDS)
+    return jnp.where(same, 1.0, 0.0)
+
+
 def attend_step_kernel(step, counts, sc_ref, *refs):
     refs = list(refs)
     make_q = step.causal and step.first
@@ -240,14 +264,13 @@
 
     groups = len(counts)
     xs = [take(count) for count in counts]
-    kaugs = take(groups)
+    segs = take(groups) if step.causal else [None] * groups
     a_ref, b_ref = take(2)
     q_ref = take(1)[0] if step.first and not make_q else None
-    seg_ref = take(1)[0] if step.first else None
     qa_in, acc_in, m_in = (None, None, None) if step.first else take(3)
     pieces = take(len(step.w.arrays))
     q_out = take(1)[0] if make_q else None
-    k_outs, v_outs, r_outs = take(groups), take(groups), take(groups)
+    k_outs, v_outs, r_outs, kaugs = take(groups), take(groups), take(groups), take(groups)
     qa_out, o_out = None, None
     if step.first and not step.last:
         qa_out = take(1)[0]
@@ -271,6 +294,7 @@
             if group == 0:
                 for slot in range(len(parts)):
                     start_all(copies(slot))
+            kaugs[group][...] = key_rows(segs[group], kaugs[group].shape[0]).T.astype(BF16)
             low = 0
             tables = a_ref[...].reshape(-1, a_ref.shape[-1])
             for x_ref in xs[group]:
@@ -300,7 +324,7 @@
             q = q_all[:, head_cols(pair)] if make_q else q_ref[:, pair_cols(pair)]
             if make_q:
                 q_out[:, pair_cols(pair)] = q
-            seg = seg_ref[...]
+            seg = query_rows(segs[0], q.shape[0])
             qt = split_pair_t((turned(q) * SCALE).astype(BF16))
             qas.append(jnp.concatenate([qt, jnp.concatenate([seg, seg], axis=1).astype(BF16)], axis=0))
             if not step.last:
@@ -344,7 +368,7 @@
             qa_out[pair] = jnp.concatenate([qas[pair][:PAIR], term_rows(-lse, qas[pair][PAIR:].astype(F32))], axis=0)
 
 
-def attend_step(step, scalars, xs, tokens, block_rows, tables, kaugs, q, seg, state):
+def attend_step(step, scalars, xs, tokens, block_rows, tables, q, state):
     width = xs[0][0].shape[1]
     pairs = width // PAIR
     keys = [block_rows * len(group) for group in xs]
@@ -358,21 +382,23 @@
     q_shape = jax.ShapeDtypeStruct((tokens, width), BF16)
     qa_shape = jax.ShapeDtypeStruct((pairs, PAIR + AUG, 2 * tokens), BF16)
     in_specs = [pl.BlockSpec((block_rows, width), lambda h, s: (0, 0))] * sum(len(group) for group in xs)
-    in_specs += [pl.BlockSpec((rows, AUG), lambda h, s: (0, 0)) for rows in keys] + [adapters, adapters]
-    args = [x for group in xs for x in group] + [*kaugs, *tables]
+    args = [x for group in xs for x in group]
+    if step.causal:
+        in_specs += [pl.BlockSpec((16, width), lambda h, s: (tokens // 16, 0))] * len(xs)
+        args += [group[0] for group in xs]
+    in_specs += [adapters, adapters]
+    args += tables
     if step.first and not make_q:
         in_specs.append(by_head)
         args.append(q)
-    if step.first:
-        in_specs.append(pl.BlockSpec((AUG, tokens), lambda h, s: (0, 0)))
-        args.append(seg)
-    else:
+    if not step.first:
         in_specs += [extended, extended, m_spec]
         args += state
     keys_by_head = [pl.BlockSpec((rows, PER * PAIR), lambda h, s: (0, h)) for rows in keys]
-    out_specs = [*keys_by_head, *keys_by_head, *[pl.BlockSpec((rows, slots * RANK), lambda h, s: (0, 0)) for rows in keys]]
+    out_specs = [*keys_by_head, *keys_by_head]
+    out_specs += [pl.BlockSpec((rows, cols), lambda h, s: (0, 0)) for cols in (slots * RANK, AUG) for rows in keys]
     kv_shapes = [jax.ShapeDtypeStruct((rows, width), BF16) for rows in keys]
-    out_shape = [*kv_shapes, *kv_shapes, *[jax.ShapeDtypeStruct((rows, slots * RANK), BF16) for rows in keys]]
+    out_shape = [*kv_shapes, *kv_shapes, *[jax.ShapeDtypeStruct((rows, cols), BF16) for cols in (slots * RANK, AUG) for rows in keys]]
     if make_q:
         out_specs.insert(0, by_head)
         out_shape.insert(0, q_shape)
@@ -404,7 +430,7 @@
     out = list(call(scalars, *args, *step.w.arrays))
     q = out.pop(0) if make_q else q
     count = len(xs)
-    return q, out[:count], out[count : 2 * count], out[2 * count : 3 * count], out[3 * count :]
+    return q, *[out[at * count : (at + 1) * count] for at in range(4)], out[4 * count :]
 
 
 def back_step_kernel(step, count, sc_ref, *refs):
@@ -667,35 +693,50 @@
     )(scalars, outs, residual, proj_down, proj_up, proj_down, proj_up, *w.arrays)
 
 
-def gelu_kernel(w, sc_ref, x_ref, a_ref, b_ref, *refs):
-    pieces, (g_ref, slope_ref, r_ref, w_ref, sems) = refs[: len(w.arrays)], refs[len(w.arrays) :]
-    copies = w.bring(pieces, sc_ref[1], 0, w_ref, sems.at[0])
-    start_all(copies)
-    x = x_ref[...]
-    hidden = low_rank(x, a_ref[0, 0])
-    r_ref[...] = hidden
-    wait_all(copies)
+def gelu_kernel(sc_ref, x_ref, a_ref, b_ref, w_in, g_ref, slope_ref, r_ref, w_ref, low, sems):
+    at = pl.program_id(0)
+    run = g_ref.shape[1]
+
+    def column(step):
+        cols = pl.ds(pl.multiple_of(step * run, run), run)
+        return pltpu.make_async_copy(w_in.at[:, cols], w_ref.at[:, cols], sems.at[step])
+
+    @pl.when(at == 0)
+    def _():
+        for step in range(w_in.shape[1] // run):
+            column(step).start()
+        low[...] = low_rank(x_ref[...], a_ref[0, 0])
+        r_ref[...] = low[...]
+
+    column(at).wait()
 
     def body(cols):
-        pre = nn(x, w_ref[:, cols]) + nn(hidden, b_ref[0, 0, :, cols])
+        across = pl.ds(pl.multiple_of(at * run, run) + cols.start, COLS)
+        pre = nn(x_ref[...], w_ref[:, across]) + nn(low[...], b_ref[0, 0, :, cols])
         phi = 0.5 * (1.0 + lax.erf(pre * 0.7071067811865476))
         g_ref[:, cols] = (pre * phi).astype(BF16)
         slope_ref[:, cols] = (phi + pre * jnp.exp(-0.5 * pre * pre) * 0.3989422804014327).astype(BF16)
 
-    each(g_ref.shape[1], COLS, body)
+    each(run, COLS, body)
 
 
 def gelu_up(scalars, x, down, up, w):
     rows, width = x.shape
     wide = up.shape[3]
+    by_column = pl.BlockSpec((rows, width), lambda c, s: (0, c))
     return pl.pallas_call(
-        functools.partial(gelu_kernel, w),
+        gelu_kernel,
         grid_spec=pltpu.PrefetchScalarGridSpec(
             num_scalar_prefetch=1,
-            grid=(1,),
-            in_specs=[WHOLE, mlp_adapter_spec(width), mlp_adapter_spec(wide), *w.specs()],
-            out_specs=[WHOLE] * 3,
-            scratch_shapes=[pltpu.VMEM((width, wide), BF16), w.sems(1)],
+            grid=(wide // width,),
+            in_specs=[
+                pl.BlockSpec((rows, width), lambda c, s: (0, 0)),
+                mlp_adapter_spec(width),
+                pl.BlockSpec((1, 1, RANK, width), lambda c, s: (0, s[2], 0, c)),
+                ANY,
+            ],
+            out_specs=[by_column, by_column, pl.BlockSpec((rows, RANK), lambda c, s: (0, 0))],
+            scratch_shapes=[pltpu.VMEM((width, wide), BF16), pltpu.VMEM((rows, RANK), BF16), pltpu.SemaphoreType.DMA((wide // width,))],
         ),
         out_shape=[
             jax.ShapeDtypeStruct((rows, wide), BF16),
@@ -712,24 +753,31 @@
 FC_TOTAL = 208
 
 
-def mlp_kernel(w_up, w_down, w_mid, sc_ref, g_ref, slope_ref, h2_ref, h2_low_ref, std2_ref, cot_ref, r1_ref, rco_ref, oc_ref,
+def mlp_kernel(w_up, w_down, w_mid, sc_ref, g_in, slope_in, h2_in, h2_low_in, std2_ref, cot_in, r1_ref, rco_ref, oc_in,
                a1_ref, b1_ref, a2_ref, b2_ref, a7_ref, b7_ref, *refs):
     ups, refs = refs[: len(w_up.arrays)], refs[len(w_up.arrays) :]
     downs, refs = refs[: len(w_down.arrays)], refs[len(w_down.arrays) :]
     mids, refs = refs[: len(w_mid.arrays)], refs[len(w_mid.arrays) :]
-    y_ref, d2_ref, doc_ref, gac_ref, grads_ref, w1, w2, wco, u, low, dpre, sem1, sem2, sem3 = refs
+    y_ref, d2_ref, doc_ref, gac_ref, grads_ref, w1, w2, wco, u, low, dpre, sem1, sem2, sem3, *local = refs
+    g_ref, slope_ref, h2_ref, h2_low_ref, cot_ref, oc_ref, sem4 = local
     rows, width = h2_ref.shape
     wide = g_ref.shape[1]
     own = sc_ref[1]
+    pairs = ((g_in, g_ref), (h2_in, h2_ref), (cot_in, cot_ref), (slope_in, slope_ref), (h2_low_in, h2_low_ref), (oc_in, oc_ref))
+    inputs = [pltpu.make_async_copy(source, target, sem4.at[at]) for at, (source, target) in enumerate(pairs)]
+    inputs[0].start()
     copies2 = w_down.bring(downs, own, 0, w2, sem2.at[0])
     copies1 = w_up.bring(ups, own, 0, w1, sem1.at[0])
     copies3 = w_mid.bring(mids, own, 1, wco, sem3.at[0])
     start_all(copies2)
+    start_all(inputs[1:])
     start_all(copies1)
     start_all(copies3)
+    inputs[0].wait()
     g = g_ref[...]
     r2 = low_rank(g, a2_ref[0, 0])
     wait_all(copies2)
+    inputs[1].wait()
 
     def second(cols):
         u[:, cols] = h2_ref[:, cols] + nn(g_ref[...], w2[:, cols]) + nn(r2, b2_ref[0, 0, :, cols])
@@ -746,7 +794,9 @@
         u[at, :] = d3
         low[at, :] = d3.astype(BF16)
 
+    inputs[2].wait()
     each(rows, ROWS, third)
+    wait_all(inputs[3:])
     d3_low = low[...]
     grads_ref[pl.ds(FC_ROWS["db2"], RANK), :] = tn(r2, d3_low).astype(BF16)
     dr2 = low_rank(d3_low, b2_ref[0, 0])
@@ -765,7 +815,7 @@
         grads_ref[pl.ds(FC_ROWS["db1"] + row, RANK), place] = tn(r1, part).astype(BF16)
         return carry
 
-    lax.fori_loop(0, wide // run, slopes, 0)
+    lax.fori_loop(0, wide // run, slopes, 0, unroll=2)
     dr1 = low_rank(dpre[...], b1_ref[0, 0])
     grads_ref[pl.ds(FC_ROWS["da1"], RANK), :] = tn(dr1, h2_low_ref[...]).astype(BF16)
     wait_all(copies1)
@@ -805,7 +855,7 @@
             num_scalar_prefetch=1,
             grid=(1,),
             in_specs=[
-                *[WHOLE] * 9,
+                *[ANY] * 4, WHOLE, ANY, WHOLE, WHOLE, ANY,
                 mlp_adapter_spec(width),
                 mlp_adapter_spec(wide),
                 mlp_adapter_spec(wide),
@@ -827,6 +877,13 @@
                 w_up.sems(1),
                 w_down.sems(1),
                 w_mid.sems(1),
+                pltpu.VMEM((rows, wide), BF16),
+                pltpu.VMEM((rows, wide), BF16),
+                pltpu.VMEM((rows, width), F32),
+                pltpu.VMEM((rows, width), BF16),
+                pltpu.VMEM((rows, width), BF16),
+                pltpu.VMEM((rows, width), BF16),
+                pltpu.SemaphoreType.DMA((6,)),
             ],
         ),
         out_shape=[
@@ -1100,17 +1157,6 @@
 
         seg_row = jnp.pad(segments.astype(BF16), ((0, 15), (0, width - tokens)))
         ext = [jnp.concatenate([x_low, seg_row], axis=0)]
-        lane = jnp.arange(AUG, dtype=jnp.int32)
-        kinds = (lane >= TERMS) & (lane < TERMS + SEG_KINDS)
-        q_seg = (kinds[:, None] & (lane[:, None] - TERMS == segments)).astype(F32)
-        free_seg = jnp.zeros((AUG, tokens), F32)
-
-        def key_aug(block):
-            seg = block[tokens, :tokens].astype(jnp.int32)
-            return jnp.where(lane[None] < TERMS, 1.0, jnp.where(kinds[None] & (lane[None] - TERMS != seg[:, None]), FAR, 0.0)).astype(BF16)
-
-        free_aug = jnp.broadcast_to((lane[None] < TERMS).astype(BF16), (span * mem_rows, AUG))
-
         a.begin()
         ext.append(turn(ext[0], 1))
         a.x, a.y, a.own, ext[1] = tie(a.x, a.y, a.own, ext[1])
@@ -1129,9 +1175,8 @@
             step = Step(f"self_{at}", w_a, (0, 1, 2) if at == 0 else (1, 2), (at, at + 1), at == 0, at == span - 2, True)
             if at:
                 ext[at], ext[at + 1], state[1] = tie(ext[at], ext[at + 1], state[1])
-            augs += [key_aug(ext[at]), key_aug(ext[at + 1])]
-            q, k, v, r, out = attend_step(step, scalars, [[ext[at]], [ext[at + 1]]], tokens, tokens, tables, augs[at:], q, q_seg, state)
-            ks, vs, rs = ks + k, vs + v, rs + r
+            q, k, v, r, aug, out = attend_step(step, scalars, [[ext[at]], [ext[at + 1]]], tokens, tokens, tables, q, state)
+            ks, vs, rs, augs = ks + k, vs + v, rs + r, augs + aug
             if at < span - 2:
                 state = out if at == 0 else [state[0], *out]
             else:
@@ -1150,10 +1195,10 @@
         qc, d.shard, *mems[1:] = tie(qc, d.shard, *mems[1:])
         d.begin()
         step = Step("cross", w_b, (3, 4), (0,), True, True, False)
-        _, (kc,), (vc,), (r_mem,), (oc, qca) = attend_step(step, scalars, [mems], tokens, mem_rows, tables, [free_aug], qc, free_seg, None)
-        oc, d.x, d.y, d.own = tie(oc, d.x, d.y, d.own)
+        _, (kc,), (vc,), (r_mem,), (free_aug,), (oc, qca) = attend_step(step, scalars, [mems], tokens, mem_rows, tables, qc, None)
+        h2, h2_low, std2, r_co = mid("mid_cross", scalars, oc, h1, 1, 7, False, *tables, w_b)
+        h2_low, d.x, d.y, d.own = tie(h2_low, d.x, d.y, d.own)
         d.forward()
-        h2, h2_low, std2, r_co = mid("mid_cross", scalars, oc, h1, 1, 7, False, *tables, w_b)
         w_c = c.result()
         g, slope, r_fc1 = gelu_up(scalars, h2_low, fc1_down, fc1_up, w_c)
         g, d.xy, d.yx, *d.near = tie(g, d.xy, d.yx, *d.near)
@@ -1185,14 +1230,13 @@
             return jnp.concatenate([values, across(values, bit)], axis=0)
 
         bits = [1 << at for at in range(chips.bit_length() - 1)]
-        state, moving, at_bit = None, None, 0
+        state, moving, waiting, at_bit = None, None, [], 0
         for at in reversed(range(span)):
             step = Step(f"self_back_{at}", w_a, (0, 1, 2) if at == 0 else (1, 2), (at,), at == span - 1, at == 0, True)
             out = back_step(step, scalars, qa, ga, q, do, ks[at], vs[at], augs[at], rs[at], [ext[at]], tokens, tables, state, d1)
             if at == 0:
                 dx, g2 = out
-                dx, g2, moving, g0, g1 = tie(dx, g2, moving, g0, g1)
-                dx = dx + moving.astype(F32)
+                g2, g0, g1, moving = tie(g2, g0, g1, moving)
             else:
                 part, *state = out
                 if at == span - 1:
@@ -1202,20 +1246,27 @@
                     for slot in range(middle + 2, span):
                         upper = turn(added(slot, upper), 1)
                     lower = added(1, lower)
+                    moving = turn(part, -1)
+                elif at == 1:
+                    waiting.append(part)
+                    state[0], moving, *waiting = tie(state[0], moving, *waiting)
+                    while len(waiting) > 1:
+                        part = (waiting.pop(0).astype(F32) + moving.astype(F32)).astype(BF16)
+                        part, state[0] = tie(part, state[0])
+                        moving = turn(part, -1)
                 else:
-                    part, state[0], moving, g0, *on = tie(part, state[0], moving, g0, *([g1] if at == 1 else []))
-                    part = (part.astype(F32) + moving.astype(F32)).astype(BF16)
-                    part, state[0] = tie(part, state[0])
-                moving = turn(part, -1)
-                if at_bit < len(bits):
+                    waiting.append(part)
+                if at == span - 2:
+                    g0, state[0] = tie(g0, state[0])
+                if at >= span - 2 and at_bit < len(bits):
                     g0 = doubled(g0, bits[at_bit])
                     at_bit += 1
-                if at == 1:
-                    while at_bit < len(bits):
-                        g0 = doubled(g0, bits[at_bit])
-                        at_bit += 1
-                    g1 = doubled(on[0][None], bits[0])
+        while at_bit < len(bits):
+            g0 = doubled(g0, bits[at_bit])
+            at_bit += 1
+
         g0 = jnp.concatenate([g0, sibling(g0)], axis=0)
+        g1 = doubled(g1[None], bits[0])
         g2 = (g2.astype(F32) + swap(g2, 1).astype(F32)).astype(BF16)
         g2, g1, g0 = tie(g2, g1, g0)
         for bit in bits[1:]:
@@ -1226,17 +1277,19 @@
         while bit < span:
             g2 = (g2.astype(F32) + swap(g2, bit).astype(F32)).astype(BF16)
             bit *= 2
-        g2, g1, lower, picks, *fcs = tie(g2, g1, lower, picks, *fcs)
-        lower = turn(lower, -1)
+        g2, g1, lower, picks, moving, *fcs = tie(g2, g1, lower, picks, moving, *fcs)
+        moving = turn((waiting[0].astype(F32) + moving.astype(F32)).astype(BF16), -1)
         g1 = jnp.concatenate([g1, sibling(g1)], axis=0)
         g2 = doubled(g2[None], bits[0])
         g2, g1, picks = tie(g2, g1, picks)
+        lower = turn(lower, -1)
         projs = proj_total(picks, (g0, g1), range(3, 8), None, proj_down.shape)
         for bit in bits[1:]:
             g2 = doubled(g2, bit)
-        g2, *projs = tie(g2, *projs)
+        g2, lower, moving, *projs = tie(g2, lower, moving, *projs)
         g2 = jnp.concatenate([g2, sibling(g2)], axis=0)
-        projs = proj_total(picks, (g2,), range(3), projs, proj_down.shape)
+        projs = list(proj_total(picks, (g2,), range(3), projs, proj_down.shape))
+        dx = dx + moving.astype(F32)
         dmem = dmem + lower.astype(F32) + upper.astype(F32)
         return (y[None], dx[None], dmem[None], *projs, *fcs)
 

time: 440 us -> 423 us (0.961)
  other arithmetic: 25.8 us -> 19.3 us
  waiting for transfers between devices: 131 us -> 125 us
  local copies, waits for them, and re-layouts: 11.5 us -> 5.85 us
    ppermute x18, waiting for transfers between devices: 70.3 us -> 55.7 us  [across(): return lax.ppermute(values, 'chip', [(i, i ^ bit) for i in range(chips)])]
    ppermute x12, waiting for transfers between devices: 45.4 us -> 58.3 us  [turn(): lax.ppermute(values, 'sp', [(i, (i + by) % span) for i in range(span)])]
  transfers between devices with their start and end apart: 48 -> 48, of which waited for: 24 -> 28; matrix products, arithmetic and copies ran while one was open for 6% -> 4% of each run, Pallas kernels for 38% -> 39%
where the time goes in v1:
time: 423 us; the launch traced here: 416 us
  Pallas kernels  197 us (47%)
  waiting for transfers between devices  125 us (30%)
  starting transfers between devices  53.5 us (13%)
  other arithmetic  19.3 us (5%)
  between operations  15.2 us (4%)
  local copies, waits for them, and re-layouts  5.85 us (1%)
    pallas_call x5, Pallas kernels, back_step(): pl.pallas_call(functools.partial(back_step_kernel, step, len(xs)), grid_s...  65.1 us
    ppermute x12, waiting for transfers between devices, turn(): lax.ppermute(values, 'sp', [(i, (i + by) % span) for i in range(span)])  58.3 us
    ppermute x18, waiting for transfers between devices, across(): return lax.ppermute(values, 'chip', [(i, i ^ bit) for i in range(chips)])  55.7 us
    pallas_call x3, Pallas kernels, attend_step(): out = list(call(scalars, *args, *step.w.arrays))  44.5 us
    pallas_call x1, Pallas kernels, mlp(): pl.pallas_call(functools.partial(mlp_kernel, w_up, w_down, w_mid), grid_s...  32.7 us
    ppermute x12, starting transfers between devices, turn(): lax.ppermute(values, 'sp', [(i, (i + by) % span) for i in range(span)])  26.3 us
    ppermute x18, starting transfers between devices, across(): return lax.ppermute(values, 'chip', [(i, i ^ bit) for i in range(chips)])  20.4 us
    pallas_call x2, Pallas kernels, mid(): pl.pallas_call(functools.partial(mid_kernel, w, part, query), grid_spec=p...  15.7 us
  transfers between devices with their start and end apart: 48, of which 28 were waited for; matrix products, arithmetic and copies ran while one was open for 4% of the time, Pallas kernels for 39%

profile of v1, /device:TPU:0, one launch (start us, length us, event | category | flops | bytes accessed | tf_op | source)
XLA Modules:
  0.0 415.8 jit_solution(6234011877726277899)
XLA Ops:
  15.7 16.9 %collective-permute-done.1.refs_9_.refs_12_.refs_14_.refs_16_.refs_17_ = bf16[384,1024]{1,0:T(8,128)(2,1)S(1)} collective-permute-done((bf16[384,1024]{1,0:T(8,128)(2,1)S(1)}, bf16[384,1024]{1,0:T(8,128)(2,1)S(1)}, u32[]{:S(2)}, u32[]{:S(2)}) %collective-permute-start.1) | collective-permute-done | bytes 786464 | tf_op jit(solution)/shard_map/ppermute | solution.py:1118
  39.3 7.8 %collective-permute-done.5.refs_13_.refs_16_.refs_18_.refs_20_.refs_21_ = bf16[192,1024]{1,0:T(8,128)(2,1)S(1)} collective-permute-done((bf16[192,1024]{1,0:T(8,128)(2,1)S(1)}, bf16[192,1024]{1,0:T(8,128)(2,1)S(1)}, u32[]{:S(2)}, u32[]{:S(2)}) %collective-permute-start.5) | collective-permute-done | bytes 393248 | tf_op jit(solution)/shard_map/ppermute | solution.py:1118
  48.3 6.9 %collective-permute-done.6.refs_0_.refs_2_.refs_10_ = bf16[400,1024]{1,0:T(8,128)(2,1)} collective-permute-done((bf16[400,1024]{1,0:T(8,128)(2,1)S(1)}, bf16[400,1024]{1,0:T(8,128)(2,1)}, u32[]{:S(2)}, u32[]{:S(2)}) %collective-permute-start.6) | collective-permute-done | bytes 819232 | tf_op jit(solution)/shard_map/ppermute | solution.py:1112
  59.3 14.0 %self_0.1 = (bf16[384,1024]{1,0:T(8,128)(2,1)}, bf16[384,1024]{1,0:T(8,128)(2,1)}, bf16[384,1024]{1,0:T(8,128)(2,1)}, bf16[384,1024]{1,0:T(8,128)(2,1)}, bf16[38...) custom-call(s32[3]{0:T(128)} %pad_add_fusion.sc_ref, ...), custom_call_target="tpu_custom_call" | custom-call | flops 27599998976 | tf_op jit(solution)/shard_map/self_0/pallas_call | solution.py:430
  73.3 7.8 %collective-permute-done.13.refs_1_.refs_3_.refs_10_ = bf16[400,1024]{1,0:T(8,128)(2,1)} collective-permute-done((bf16[400,1024]{1,0:T(8,128)(2,1)}, bf16[400,1024]{1,0:T(8,128)(2,1)}, u32[]{:S(2)}, u32[]{:S(2)}) %collective-permute-start.13) | collective-permute-done | bytes 819232 | tf_op jit(solution)/shard_map/ppermute | solution.py:1112
  81.0 7.1 %collective-permute-done.11.refs_3_.refs_10_.refs_12_.refs_17_ = bf16[640,1024]{1,0:T(8,128)(2,1)S(1)} collective-permute-done((bf16[640,1024]{1,0:T(8,128)(2,1)}, bf16[640,1024]{1,0:T(8,128)(2,1)S(1)}, u32[]{:S(2)}, u32[]{:S(2)}) %collective-permute-start.11) | collective-permute-done | bytes 1310752 | tf_op jit(solution)/shard_map/ppermute | solution.py:1118
  95.6 7.1 %self_2.1 = (bf16[384,1024]{1,0:T(8,128)(2,1)}, bf16[384,1024]{1,0:T(8,128)(2,1)}, bf16[384,1024]{1,0:T(8,128)(2,1)}, bf16[384,1024]{1,0:T(8,128)(2,1)}, bf16[38...) custom-call(s32[3]{0:T(128)} %pad_add_fusion.sc_ref, ...), custom_call_target="tpu_custom_call" | custom-call | flops 27599998976 | tf_op jit(solution)/shard_map/self_2/pallas_call | solution.py:430
  105.3 11.3 %collective-permute-done.14.refs_1_.refs_11_ = bf16[256,1024]{1,0:T(8,128)(2,1)} collective-permute-done((bf16[256,1024]{1,0:T(8,128)(2,1)}, bf16[256,1024]{1,0:T(8,128)(2,1)}, u32[]{:S(2)}, u32[]{:S(2)}) %collective-permute-start.14) | collective-permute-done | bytes 524320 | tf_op jit(solution)/shard_map/ppermute | solution.py:1112
  126.2 8.4 %mid.1 = (f32[384,1024]{1,0:T(8,128)}, bf16[384,1024]{1,0:T(8,128)(2,1)}, f32[384,1]{1,0:T(8,128)}, bf16[384,32]{1,0:T(8,128)(2,1)}, bf16[384,1024]{1,0:T(8,128)(2,1)}) custom-call(s32[3]{0:T(128)} %pad_add_fusion.sc_ref, bf16[384,1024]{1,0:T(8,128)(2,1)} %get-tuple-element.180.o_ref, bf16[384,1024]{1,0:T(8,128)(2,1)} %bitcast.19, ...), custom_call_target="tpu_custom_call" | custom-call | flops 1150000000 | tf_op jit(solution)/shard_map/mid/pallas_call | solution.py:680
  140.3 23.5 %cross.1 = (bf16[1024,1024]{1,0:T(8,128)(2,1)}, bf16[1024,1024]{1,0:T(8,128)(2,1)}, bf16[1024,32]{1,0:T(8,128)(2,1)}, bf16[1024,16]{1,0:T(8,128)(2,1)}, bf16[384...) custom-call(s32[3]{0:T(128)} %pad_add_fusion.sc_ref, bf16[256,1024]{1,0:T(8,128)(2,1)} %bitcast.2.refs_0_.refs_10_, ...), custom_call_target="tpu_custom_call" | custom-call | flops 36800000000 | tf_op jit(solution)/shard_map/cross/pallas_call | solution.py:430
  163.8 7.3 %mid_cross.1 = (f32[384,1024]{1,0:T(8,128)}, bf16[384,1024]{1,0:T(8,128)(2,1)}, f32[384,1]{1,0:T(8,128)}, bf16[384,16]{1,0:T(8,128)(2,1)}) custom-call(s32[3]{0:T(128)} %pad_add_fusion.sc_ref, bf16[384,1024]{1,0:T(8,128)(2,1)} %get-tuple-element.192.o_ref.oc_in, f32[384,1024]{1,0:T(8,128)} %get-tuple-element.193.x_ref.h1_ref, ...), custom_call_target="tpu_custom_call" | custom-call | flops 1150000000 | tf_op jit(solution)/shard_map/mid_cross/pallas_call | solution.py:680
  176.6 11.8 %gelu_up.1 = (bf16[384,4096]{1,0:T(8,128)(2,1)}, bf16[384,4096]{1,0:T(8,128)(2,1)}, bf16[384,16]{1,0:T(8,128)(2,1)}) custom-call(s32[3]{0:T(128)} %pad_add_fusion.sc_ref, bf16[384,1024]{1,0:T(8,128)(2,1)} %get-tuple-element.196.x_ref.h2_low_in, bf16[1,8,16,1024]{3,2,1,0:T(8,128)(2,1)} %a1_ref.1, bf16[1,8,16,4096]{3,2,1,0:T(8,128)(2,1)} %b1_ref.1, ...), custom_call_target="tpu_custom_call" | custom-call | flops 17250000896 | tf_op jit(solution)/shard_map/gelu_up/pallas_call | solution.py:727
  193.6 32.7 %mlp.1 = (bf16[384,1024]{1,0:T(8,128)(2,1)}, f32[384,1024]{1,0:T(8,128)}, bf16[384,1024]{1,0:T(8,128)(2,1)}, bf16[8,144,768]{2,1,0:T(8,128)(2,1)}, bf16[208,1024]{1,0:T(8,128)(2,1)}) custom-call(s32[3]{0:T(128)} %pad_add_fusion.sc_ref, bf16[384,4096]{1,0:T(8,128)(2,1)} %get-tuple-element.201.g_in, bf16[384,4096]{1,0:T(8,128)(2,1)} %get-tuple-element.202.slope_in, ...), custom_call_target="tpu_custom_call" | custom-call | flops 37950001152 | tf_op jit(solution)/shard_map/mlp/pallas_call | solution.py:852
  226.4 28.4 %cross_back.1 = (f32[256,1024]{1,0:T(8,128)}, bf16[768,1024]{1,0:T(8,128)(2,1)}, bf16[384,1024]{1,0:T(8,128)(2,1)}, bf16[64,1024]{1,0:T(8,128)(2,1)}) custom-call(s32[3]{0:T(128)} %pad_add_fusion.sc_ref, bf16[8,144,768]{2,1,0:T(8,128)(2,1)} %get-tuple-element.213.refs_0_, bf16[8,144,768]{2,1,0:T(8,128)(2,1)} %get-tuple-element.214.refs_1_, ...), custom_call_target="tpu_custom_call" | custom-call | flops 49066668032 | tf_op jit(solution)/shard_map/cross_back/pallas_call | solution.py:607
  260.0 10.7 %mid_back.1 = (f32[384,1024]{1,0:T(8,128)}, bf16[384,1024]{1,0:T(8,128)(2,1)}, bf16[8,144,768]{2,1,0:T(8,128)(2,1)}, bf16[64,1024]{1,0:T(8,128)(2,1)}) custom-call(s32[3]{0:T(128)} %pad_add_fusion.sc_ref, bf16[384,1024]{1,0:T(8,128)(2,1)} %get-tuple-element.220.dqc_ref, f32[384,1024]{1,0:T(8,128)} %get-tuple-element.221.d2_ref, ...), custom_call_target="tpu_custom_call" | custom-call | flops 1150000000 | tf_op jit(solution)/shard_map/mid_back/pallas_call | solution.py:945
  270.7 6.4 %self_back_3.1 = (bf16[384,1024]{1,0:T(8,128)(2,1)}, f32[8,128,384]{2,1,0:T(8,128)}, f32[64,1024]{1,0:T(8,128)}) custom-call(s32[3]{0:T(128)} %pad_add_fusion.sc_ref, bf16[8,144,768]{2,1,0:T(8,128)(2,1)} %get-tuple-element.212.refs_0_, bf16[8,144,768]{2,1,0:T(8,128)(2,1)} %get-tuple-element.225.refs_1_, bf16[384,1024]{1,0:T(8,128)(2,1)} %get-tuple-element.226.refs_2_, ...), custom_call_target="tpu_custom_call" | custom-call | flops 18400000000 | tf_op jit(solution)/shard_map/self_back_3/pallas_call | solution.py:607
  278.5 6.1 %collective-permute-done.29 = bf16[256,1024]{1,0:T(8,128)(2,1)S(1)} collective-permute-done((bf16[256,1024]{1,0:T(8,128)(2,1)S(1)}, bf16[256,1024]{1,0:T(8,128)(2,1)S(1)}, u32[]{:S(2)}, u32[]{:S(2)}) %collective-permute-start.29) | collective-permute-done | bytes 524320 | tf_op jit(solution)/shard_map/ppermute | solution.py:1112
  288.4 7.2 %self_back_2.1 = (bf16[384,1024]{1,0:T(8,128)(2,1)}, f32[8,128,384]{2,1,0:T(8,128)}, f32[64,1024]{1,0:T(8,128)}) custom-call(s32[3]{0:T(128)} %pad_add_fusion.sc_ref, bf16[8,144,768]{2,1,0:T(8,128)(2,1)} %get-tuple-element.212.refs_0_, bf16[8,144,768]{2,1,0:T(8,128)(2,1)} %get-tuple-element.225.refs_1_, bf16[384,1024]{1,0:T(8,128)(2,1)} %get-tuple-element.226.refs_2_, ...), custom_call_target="tpu_custom_call" | custom-call | flops 18400000000 | tf_op jit(solution)/shard_map/self_back_2/pallas_call | solution.py:607
  297.3 6.8 %self_back_1.1 = (bf16[384,1024]{1,0:T(8,128)(2,1)}, f32[8,128,384]{2,1,0:T(8,128)}, f32[64,1024]{1,0:T(8,128)}) custom-call(s32[3]{0:T(128)} %pad_add_fusion.sc_ref, bf16[8,144,768]{2,1,0:T(8,128)(2,1)} %get-tuple-element.212.refs_0_, bf16[8,144,768]{2,1,0:T(8,128)(2,1)} %get-tuple-element.225.refs_1_, bf16[384,1024]{1,0:T(8,128)(2,1)} %get-tuple-element.226.refs_2_, ...), custom_call_target="tpu_custom_call" | custom-call | flops 18400000000 | tf_op jit(solution)/shard_map/self_back_1/pallas_call | solution.py:607
  310.4 9.5 %collective-permute-start.33 = (bf16[384,1024]{1,0:T(8,128)(2,1)}, bf16[384,1024]{1,0:T(8,128)(2,1)}, u32[]{:S(2)}, u32[]{:S(2)}) collective-permute-start(bf16[384,1024]{1,0:T(8,128)(2,1)} %add_convert_fusion.1), channel_id=1, source_target_pairs={{0,3},{1,0},{2,1},{3,2},{4,7},{5,4},{6,5},{7,6},{8,11},{9,8},{10,9... | collective-permute-start | bytes 2359304 | tf_op jit(solution)/shard_map/ppermute | solution.py:1112
  319.9 16.4 %self_back_0.1 = (f32[384,1024]{1,0:T(8,128)}, bf16[96,1024]{1,0:T(8,128)(2,1)}) custom-call(s32[3]{0:T(128)} %pad_add_fusion.sc_ref, bf16[8,144,768]{2,1,0:T(8,128)(2,1)} %get-tuple-element.212.refs_0_, bf16[8,144,768]{2,1,0:T(8,128)(2,1)} %get-tuple-element.225.refs_1_, bf16[384,1024]{1,0:T(8,128)(2,1)} %get-tuple-element.226.refs_2_, ...), custom_call_target="tpu_custom_call" | custom-call | flops 18400000000 | tf_op jit(solution)/shard_map/self_back_0/pallas_call | solution.py:607
  357.0 5.6 %fc_total.1 = (f32[1,8,16,1024]{3,2,1,0:T(8,128)}, f32[1,8,16,4096]{3,2,1,0:T(8,128)}, f32[1,8,16,4096]{3,2,1,0:T(8,128)}, f32[1,8,16,1024]{3,2,1,0:T(8,128)}) custom-call(s32[8]{0:T(128)} %convert_reduce_fusion.picks_ref, bf16[8,208,1024]{2,1,0:T(8,128)(2,1)} %copy-done.5), custom_call_target="tpu_custom_call" | custom-call | flops 6899999744 | tf_op jit(solution)/shard_map/fc_total/pallas_call | solution.py:991
  379.0 6.7 %proj_total_3.1 = (f32[1,8,8,16,1024]{4,3,2,1,0:T(8,128)}, f32[1,8,8,16,1024]{4,3,2,1,0:T(8,128)}) custom-call(s32[8]{0:T(128)} %convert_reduce_fusion.picks_ref, bf16[8,208,1024]{2,1,0:T(8,128)(2,1)} %copy-done.5, bf16[8,128,1024]{2,1,0:T(8,128)(2,1)} %pad_maximum_fusion.3.refs_1_), custom_call_target="tpu_custom_call" | custom-call | flops 8049999872 | tf_op jit(solution)/shard_map/proj_total_3/pallas_call | solution.py:1036
  388.9 11.9 %collective-permute-done.43 = bf16[384,1024]{1,0:T(8,128)(2,1)S(1)} collective-permute-done((bf16[384,1024]{1,0:T(8,128)(2,1)S(1)}, bf16[384,1024]{1,0:T(8,128)(2,1)S(1)}, u32[]{:S(2)}, u32[]{:S(2)}) %collective-permute-start.43) | collective-permute-done | bytes 786464 | tf_op jit(solution)/shard_map/ppermute | solution.py:1112
  (196 shorter events, 122.5 us)
Async XLA Ops:
  7.2 169.4 %all-gather.2.cloned.1.call-start = ((), (), s32[]{:S(2)}) async-start(), calls=%async_computation | async-start | bytes 9437184 | tf_op jit(solution)/shard_map/all_gather | solution.py:1126
  9.2 24.5 %collective-permute-start.3 = (bf16[400,1024]{1,0:T(8,128)(2,1)S(1)}, bf16[400,1024]{1,0:T(8,128)(2,1)S(1)}, u32[]{:S(2)}, u32[]{:S(2)}) collective-permute-start(bf16[400,1024]{1,0:T(8,128)(2,1)S(1)} %fusion.1.refs_0_.refs_2_.refs_10_), channel_id=1, source_target_pairs={{0,1},{1,2},{2,3},{3,0},{4,5},{5,6},{6,7},{7,4},{8,9},{9,10},{10,1... | collective-permute-start | bytes 2457608 | tf_op jit(solution)/shard_map/ppermute | solution.py:1112
  12.6 20.0 %collective-permute-start.1 = (bf16[384,1024]{1,0:T(8,128)(2,1)S(1)}, bf16[384,1024]{1,0:T(8,128)(2,1)S(1)}, u32[]{:S(2)}, u32[]{:S(2)}) collective-permute-start(bf16[384,1024]{1,0:T(8,128)(2,1)S(1)} %bitcast.23), channel_id=1, source_target_pairs={{0,16},{8,24},{16,0},{24,8},{1,17},{9,25},{17,1},{25,9},{2,18},{10... | collective-permute-start | bytes 2359304 | tf_op jit(solution)/shard_map/ppermute | solution.py:1118
  14.2 19.6 %collective-permute-start = (bf16[384,1024]{1,0:T(8,128)(2,1)S(1)}, bf16[384,1024]{1,0:T(8,128)(2,1)S(1)}, u32[]{:S(2)}, u32[]{:S(2)}) collective-permute-start(bf16[384,1024]{1,0:T(8,128)(2,1)S(1)} %bitcast.24), channel_id=1, source_target_pairs={{0,8},{8,0},{16,24},{24,16},{1,9},{9,1},{17,25},{25,17},{2,10},{10... | collective-permute-start | bytes 2359304 | tf_op jit(solution)/shard_map/ppermute | solution.py:1118
  33.8 21.4 %collective-permute-start.6 = (bf16[400,1024]{1,0:T(8,128)(2,1)S(1)}, bf16[400,1024]{1,0:T(8,128)(2,1)}, u32[]{:S(2)}, u32[]{:S(2)}) collective-permute-start(bf16[400,1024]{1,0:T(8,128)(2,1)S(1)} %collective-permute-done.3.refs_1_.refs_3_.refs_10_), channel_id=1, source_target_pairs={{0,1},{1,2},{2,3},{3,0},{4,5},{5,6},{6,7},{7,4},{8,9},{9,10},{10,1... | collective-permute-start | bytes 2457608 | tf_op jit(solution)/shard_map/ppermute | solution.py:1112
  56.7 24.3 %collective-permute-start.12 = (bf16[640,1024]{1,0:T(8,128)(2,1)}, bf16[640,1024]{1,0:T(8,128)(2,1)}, u32[]{:S(2)}, u32[]{:S(2)}) collective-permute-start(bf16[640,1024]{1,0:T(8,128)(2,1)} %pad_maximum_fusion.6.refs_0_.refs_7_.refs_9_.refs_14_), channel_id=1, source_target_pairs={{0,4},{4,0},{1,5},{5,1},{2,6},{6,2},{3,7},{7,3},{8,12},{12,8},{9,1... | collective-permute-start | bytes 3932168 | tf_op jit(solution)/shard_map/ppermute | solution.py:1121
  57.2 30.9 %collective-permute-start.11 = (bf16[640,1024]{1,0:T(8,128)(2,1)}, bf16[640,1024]{1,0:T(8,128)(2,1)S(1)}, u32[]{:S(2)}, u32[]{:S(2)}) collective-permute-start(bf16[640,1024]{1,0:T(8,128)(2,1)} %pad_maximum_fusion.6.refs_0_.refs_7_.refs_9_.refs_14_), channel_id=1, source_target_pairs={{0,16},{8,24},{16,0},{24,8},{1,17},{9,25},{17,1},{25,9},{2,18},{10... | collective-permute-start | bytes 3932168 | tf_op jit(solution)/shard_map/ppermute | solution.py:1118
  57.8 30.7 %collective-permute-start.10 = (bf16[640,1024]{1,0:T(8,128)(2,1)}, bf16[640,1024]{1,0:T(8,128)(2,1)S(1)}, u32[]{:S(2)}, u32[]{:S(2)}) collective-permute-start(bf16[640,1024]{1,0:T(8,128)(2,1)} %pad_maximum_fusion.6.refs_0_.refs_7_.refs_9_.refs_14_), channel_id=1, source_target_pairs={{0,8},{8,0},{16,24},{24,16},{1,9},{9,1},{17,25},{25,17},{2,10},{10... | collective-permute-start | bytes 3932168 | tf_op jit(solution)/shard_map/ppermute | solution.py:1118
  59.3 21.7 %collective-permute-start.13 = (bf16[400,1024]{1,0:T(8,128)(2,1)}, bf16[400,1024]{1,0:T(8,128)(2,1)}, u32[]{:S(2)}, u32[]{:S(2)}) collective-permute-start(bf16[400,1024]{1,0:T(8,128)(2,1)} %collective-permute-done.6.refs_0_.refs_2_.refs_10_), channel_id=1, source_target_pairs={{0,1},{1,2},{2,3},{3,0},{4,5},{5,6},{6,7},{7,4},{8,9},{9,10},{10,1... | collective-permute-start | bytes 2457608 | tf_op jit(solution)/shard_map/ppermute | solution.py:1112
  88.5 189.3 %all-reduce.4.cloned.1.call-start = ((), (), s32[]{:S(2)}) async-start(), calls=%async_computation.1 | async-start | bytes 851968 | tf_op jit(solution)/shard_map/psum | solution.py:1211
  90.5 31.4 %collective-permute-start.18 = (bf16[1280,1024]{1,0:T(8,128)(2,1)}, bf16[1280,1024]{1,0:T(8,128)(2,1)}, u32[]{:S(2)}, u32[]{:S(2)}) collective-permute-start(bf16[1280,1024]{1,0:T(8,128)(2,1)} %pad_maximum_fusion.1), channel_id=1, source_target_pairs={{0,4},{4,0},{1,5},{5,1},{2,6},{6,2},{3,7},{7,3},{8,12},{12,8},{9,1... | collective-permute-start | bytes 7864328 | tf_op jit(solution)/shard_map/ppermute | solution.py:1121
  91.0 25.6 %collective-permute-start.14 = (bf16[256,1024]{1,0:T(8,128)(2,1)}, bf16[256,1024]{1,0:T(8,128)(2,1)}, u32[]{:S(2)}, u32[]{:S(2)}) collective-permute-start(bf16[256,1024]{1,0:T(8,128)(2,1)} %bitcast.2.refs_0_.refs_10_), channel_id=1, source_target_pairs={{0,1},{1,2},{2,3},{3,0},{4,5},{5,6},{6,7},{7,4},{8,9},{9,10},{10,1... | collective-permute-start | bytes 1572872 | tf_op jit(solution)/shard_map/ppermute | solution.py:1112
  92.8 27.9 %collective-permute-start.17 = (bf16[320,1024]{1,0:T(8,128)(2,1)S(1)}, bf16[320,1024]{1,0:T(8,128)(2,1)S(1)}, u32[]{:S(2)}, u32[]{:S(2)}) collective-permute-start(bf16[320,1024]{1,0:T(8,128)(2,1)S(1)} %slice.41), channel_id=1, source_target_pairs={{0,8},{8,0},{16,24},{24,16},{1,9},{9,1},{17,25},{25,17},{2,10},{10... | collective-permute-start | bytes 1966088 | tf_op jit(solution)/shard_map/ppermute | solution.py:1118
  94.3 27.5 %collective-permute-start.16 = (bf16[320,1024]{1,0:T(8,128)(2,1)S(1)}, bf16[320,1024]{1,0:T(8,128)(2,1)S(1)}, u32[]{:S(2)}, u32[]{:S(2)}) collective-permute-start(bf16[320,1024]{1,0:T(8,128)(2,1)S(1)} %slice.40), channel_id=1, source_target_pairs={{0,16},{8,24},{16,0},{24,8},{1,17},{9,25},{17,1},{25,9},{2,18},{10... | collective-permute-start | bytes 1966088 | tf_op jit(solution)/shard_map/ppermute | solution.py:1118
  138.5 32.6 %collective-permute-start.23 = (bf16[512,1024]{1,0:T(8,128)(2,1)S(1)}, bf16[512,1024]{1,0:T(8,128)(2,1)}, u32[]{:S(2)}, u32[]{:S(2)}) collective-permute-start(bf16[512,1024]{1,0:T(8,128)(2,1)S(1)} %bitcast.39), channel_id=1, source_target_pairs={{0,4},{4,0},{1,5},{5,1},{2,6},{6,2},{3,7},{7,3},{8,12},{12,8},{9,1... | collective-permute-start | bytes 3145736 | tf_op jit(solution)/shard_map/ppermute | solution.py:1121
  138.5 34.0 %collective-permute-start.22 = (bf16[512,1024]{1,0:T(8,128)(2,1)S(1)}, bf16[512,1024]{1,0:T(8,128)(2,1)S(1)}, u32[]{:S(2)}, u32[]{:S(2)}) collective-permute-start(bf16[512,1024]{1,0:T(8,128)(2,1)S(1)} %bitcast.40), channel_id=1, source_target_pairs={{0,16},{8,24},{16,0},{24,8},{1,17},{9,25},{17,1},{25,9},{2,18},{10... | collective-permute-start | bytes 3145736 | tf_op jit(solution)/shard_map/ppermute | solution.py:1118
  139.8 32.7 %collective-permute-start.21 = (bf16[512,1024]{1,0:T(8,128)(2,1)S(1)}, bf16[512,1024]{1,0:T(8,128)(2,1)S(1)}, u32[]{:S(2)}, u32[]{:S(2)}) collective-permute-start(bf16[512,1024]{1,0:T(8,128)(2,1)S(1)} %bitcast.41), channel_id=1, source_target_pairs={{0,8},{8,0},{16,24},{24,16},{1,9},{9,1},{17,25},{25,17},{2,10},{10... | collective-permute-start | bytes 3145736 | tf_op jit(solution)/shard_map/ppermute | solution.py:1118
  226.3 110.1 %all-reduce.6.cloned.1.call-start = ((), (), s32[]{:S(2)}) async-start(), calls=%async_computation.2 | async-start | bytes 524288 | tf_op jit(solution)/shard_map/psum | solution.py:1226
  256.1 22.4 %collective-permute-start.30 = (bf16[256,1024]{1,0:T(8,128)(2,1)S(1)}, bf16[256,1024]{1,0:T(8,128)(2,1)S(1)}, u32[]{:S(2)}, u32[]{:S(2)}) collective-permute-start(bf16[256,1024]{1,0:T(8,128)(2,1)S(1)} %get-tuple-element.307), channel_id=1, source_target_pairs={{0,1},{1,2},{2,3},{3,0},{4,5},{5,6},{6,7},{7,4},{8,9},{9,10},{10,1... | collective-permute-start | bytes 1572872 | tf_op jit(solution)/shard_map/ppermute | solution.py:1112
  257.6 26.9 %collective-permute-start.29 = (bf16[256,1024]{1,0:T(8,128)(2,1)S(1)}, bf16[256,1024]{1,0:T(8,128)(2,1)S(1)}, u32[]{:S(2)}, u32[]{:S(2)}) collective-permute-start(bf16[256,1024]{1,0:T(8,128)(2,1)S(1)} %get-tuple-element.308), channel_id=1, source_target_pairs={{0,3},{1,0},{2,1},{3,2},{4,7},{5,4},{6,5},{7,6},{8,11},{9,8},{10,9... | collective-permute-start | bytes 1572872 | tf_op jit(solution)/shard_map/ppermute | solution.py:1112
  284.6 24.7 %collective-permute-start.31 = (bf16[384,1024]{1,0:T(8,128)(2,1)}, bf16[384,1024]{1,0:T(8,128)(2,1)S(1)}, u32[]{:S(2)}, u32[]{:S(2)}) collective-permute-start(bf16[384,1024]{1,0:T(8,128)(2,1)} %get-tuple-element.257), channel_id=1, source_target_pairs={{0,3},{1,0},{2,1},{3,2},{4,7},{5,4},{6,5},{7,6},{8,11},{9,8},{10,9... | collective-permute-start | bytes 2359304 | tf_op jit(solution)/shard_map/ppermute | solution.py:1112
  295.7 40.5 %collective-permute-start.32 = (bf16[2,208,1024]{2,1,0:T(8,128)(2,1)S(1)}, bf16[2,208,1024]{2,1,0:T(8,128)(2,1)S(1)}, u32[]{:S(2)}, u32[]{:S(2)}) collective-permute-start(bf16[2,208,1024]{2,1,0:T(8,128)(2,1)S(1)} %pad_maximum_fusion.10), channel_id=1, source_target_pairs={{0,16},{8,24},{16,0},{24,8},{1,17},{9,25},{17,1},{25,9},{2,18},{10... | collective-permute-start | bytes 2555912 | tf_op jit(solution)/shard_map/ppermute | solution.py:1118
  310.4 28.7 %collective-permute-start.33 = (bf16[384,1024]{1,0:T(8,128)(2,1)}, bf16[384,1024]{1,0:T(8,128)(2,1)}, u32[]{:S(2)}, u32[]{:S(2)}) collective-permute-start(bf16[384,1024]{1,0:T(8,128)(2,1)} %add_convert_fusion.1), channel_id=1, source_target_pairs={{0,3},{1,0},{2,1},{3,2},{4,7},{5,4},{6,5},{7,6},{8,11},{9,8},{10,9... | collective-permute-start | bytes 2359304 | tf_op jit(solution)/shard_map/ppermute | solution.py:1112
  371.6 29.2 %collective-permute-start.43 = (bf16[384,1024]{1,0:T(8,128)(2,1)S(1)}, bf16[384,1024]{1,0:T(8,128)(2,1)S(1)}, u32[]{:S(2)}, u32[]{:S(2)}) collective-permute-start(bf16[384,1024]{1,0:T(8,128)(2,1)S(1)} %add_convert_fusion), channel_id=1, source_target_pairs={{0,3},{1,0},{2,1},{3,2},{4,7},{5,4},{6,5},{7,6},{8,11},{9,8},{10,9... | collective-permute-start | bytes 2359304 | tf_op jit(solution)/shard_map/ppermute | solution.py:1112
  (59 other events, 557.6 us)
Sparse Core Ops, SparseCore 0:
  88.6 71.9 all-gather.1
  226.4 48.5 all-reduce.3
  278.0 53.5 all-reduce.5

commit v2 on v1

--- a/solution.py
+++ b/solution.py
@@ -1084,7 +1084,7 @@
 class Whole:
     def __init__(self, shard, parts, shards, gather):
         self.shard, self.parts, self.shards, self.gather = shard, parts, shards, gather
-        self.x = self.y = self.own = self.xy = self.yx = shard
+        self.x = self.y = self.own = self.xy = self.yx = self.far = shard
         self.near = []
 
     def begin(self):
@@ -1162,9 +1162,10 @@
         a.x, a.y, a.own, ext[1] = tie(a.x, a.y, a.own, ext[1])
         a.forward()
         ext.append(turn(ext[1], 1))
-        a.xy, a.yx, b.shard, ext[2], *a.near = tie(a.xy, a.yx, b.shard, ext[2], *a.near)
+        a.xy, a.yx, b.shard, *a.near = tie(a.xy, a.yx, b.shard, *a.near)
         a.share()
         b.begin()
+        a.far, ext[2] = tie(a.far, ext[2])
         while len(ext) < span:
             ext.append(turn(ext[-1], 1))
         w_a = a.result()
@@ -1222,6 +1223,7 @@
         middle = span // 2
         lower, upper = turn(mem_part(middle), -1), turn(mem_part(middle + 1), 1)
         d1, do, ga, mid_grads = mid_back(scalars, dqc, d2, h1, h1_low, std1, r_mid, o, *tables, w_b)
+        ga, g0 = tie(ga, g0)
         g0, g1 = tie(g0, jnp.concatenate([mid_grads, cross_grads], axis=0))
         g1 = lax.psum(g1, "sp")
         g0 = g0[None]
@@ -1249,7 +1251,7 @@
                     moving = turn(part, -1)
                 elif at == 1:
                     waiting.append(part)
-                    state[0], moving, *waiting = tie(state[0], moving, *waiting)
+                    state[0], moving, lower, *waiting = tie(state[0], moving, lower, *waiting)
                     while len(waiting) > 1:
                         part = (waiting.pop(0).astype(F32) + moving.astype(F32)).astype(BF16)
                         part, state[0] = tie(part, state[0])
@@ -1257,7 +1259,8 @@
                 else:
                     waiting.append(part)
                 if at == span - 2:
-                    g0, state[0] = tie(g0, state[0])
+                    g0, state[0], lower = tie(g0, state[0], lower)
+                    lower = turn(lower, -1)
                 if at >= span - 2 and at_bit < len(bits):
                     g0 = doubled(g0, bits[at_bit])
                     at_bit += 1
@@ -1277,16 +1280,15 @@
         while bit < span:
             g2 = (g2.astype(F32) + swap(g2, bit).astype(F32)).astype(BF16)
             bit *= 2
-        g2, g1, lower, picks, moving, *fcs = tie(g2, g1, lower, picks, moving, *fcs)
+        g2, g1, picks, moving, *fcs = tie(g2, g1, picks, moving, *fcs)
         moving = turn((waiting[0].astype(F32) + moving.astype(F32)).astype(BF16), -1)
         g1 = jnp.concatenate([g1, sibling(g1)], axis=0)
         g2 = doubled(g2[None], bits[0])
         g2, g1, picks = tie(g2, g1, picks)
-        lower = turn(lower, -1)
         projs = proj_total(picks, (g0, g1), range(3, 8), None, proj_down.shape)
         for bit in bits[1:]:
             g2 = doubled(g2, bit)
-        g2, lower, moving, *projs = tie(g2, lower, moving, *projs)
+        g2, moving, *projs = tie(g2, moving, *projs)
         g2 = jnp.concatenate([g2, sibling(g2)], axis=0)
         projs = list(proj_total(picks, (g2,), range(3), projs, proj_down.shape))
         dx = dx + moving.astype(F32)

time: 423 us -> 416 us (0.983)
  waiting for transfers between devices: 125 us -> 110 us
    ppermute x12, waiting for transfers between devices: 58.3 us -> 38.8 us  [turn(): lax.ppermute(values, 'sp', [(i, (i + by) % span) for i in range(span)])]
  transfers between devices with their start and end apart: 48 -> 48, of which waited for: 28 -> 28; matrix products, arithmetic and copies ran while one was open for 4% -> 5% of each run, Pallas kernels for 39% -> 39%
where the time goes in v2:
time: 416 us; the launch traced here: 409 us
  Pallas kernels  198 us (48%)
  waiting for transfers between devices  110 us (26%)
  starting transfers between devices  55.5 us (13%)
  other arithmetic  22.8 us (5%)
  between operations  15.2 us (4%)
  local copies, waits for them, and re-layouts  7.87 us (2%)
    pallas_call x5, Pallas kernels, back_step(): pl.pallas_call(functools.partial(back_step_kernel, step, len(xs)), grid_s...  64.5 us
    ppermute x18, waiting for transfers between devices, across(): return lax.ppermute(values, 'chip', [(i, i ^ bit) for i in range(chips)])  53.5 us
    pallas_call x3, Pallas kernels, attend_step(): out = list(call(scalars, *args, *step.w.arrays))  44.7 us
    ppermute x12, waiting for transfers between devices, turn(): lax.ppermute(values, 'sp', [(i, (i + by) % span) for i in range(span)])  38.8 us
    pallas_call x1, Pallas kernels, mlp(): pl.pallas_call(functools.partial(mlp_kernel, w_up, w_down, w_mid), grid_s...  32.7 us
    ppermute x12, starting transfers between devices, turn(): lax.ppermute(values, 'sp', [(i, (i + by) % span) for i in range(span)])  27.9 us
    ppermute x18, starting transfers between devices, across(): return lax.ppermute(values, 'chip', [(i, i ^ bit) for i in range(chips)])  21.3 us
    pallas_call x2, Pallas kernels, mid(): pl.pallas_call(functools.partial(mid_kernel, w, part, query), grid_spec=p...  16 us
  transfers between devices with their start and end apart: 48, of which 28 were waited for; matrix products, arithmetic and copies ran while one was open for 5% of the time, Pallas kernels for 39%

profile of v2, /device:TPU:0, one launch (start us, length us, event | category | flops | bytes accessed | tf_op | source)
XLA Modules:
  0.0 408.6 jit_solution(2749464002456848720)
XLA Ops:
  15.7 16.9 %collective-permute-done.1.refs_9_.refs_12_.refs_14_.refs_16_.refs_17_ = bf16[384,1024]{1,0:T(8,128)(2,1)S(1)} collective-permute-done((bf16[384,1024]{1,0:T(8,128)(2,1)S(1)}, bf16[384,1024]{1,0:T(8,128)(2,1)S(1)}, u32[]{:S(2)}, u32[]{:S(2)}) %collective-permute-start.1) | collective-permute-done | bytes 786464 | tf_op jit(solution)/shard_map/ppermute | solution.py:1118
  39.2 6.3 %collective-permute-done.5.refs_13_.refs_16_.refs_18_.refs_20_.refs_21_ = bf16[192,1024]{1,0:T(8,128)(2,1)S(1)} collective-permute-done((bf16[192,1024]{1,0:T(8,128)(2,1)S(1)}, bf16[192,1024]{1,0:T(8,128)(2,1)S(1)}, u32[]{:S(2)}, u32[]{:S(2)}) %collective-permute-start.5) | collective-permute-done | bytes 393248 | tf_op jit(solution)/shard_map/ppermute | solution.py:1118
  50.4 9.0 %collective-permute-done.9.refs_0_.refs_2_.refs_10_ = bf16[400,1024]{1,0:T(8,128)(2,1)} collective-permute-done((bf16[400,1024]{1,0:T(8,128)(2,1)}, bf16[400,1024]{1,0:T(8,128)(2,1)}, u32[]{:S(2)}, u32[]{:S(2)}) %collective-permute-start.9) | collective-permute-done | bytes 819232 | tf_op jit(solution)/shard_map/ppermute | solution.py:1112
  59.4 14.0 %self_0.1 = (bf16[384,1024]{1,0:T(8,128)(2,1)}, bf16[384,1024]{1,0:T(8,128)(2,1)}, bf16[384,1024]{1,0:T(8,128)(2,1)}, bf16[384,1024]{1,0:T(8,128)(2,1)}, bf16[38...) custom-call(s32[3]{0:T(128)} %pad_add_fusion.sc_ref, ...), custom_call_target="tpu_custom_call" | custom-call | flops 27599998976 | tf_op jit(solution)/shard_map/self_0/pallas_call | solution.py:430
  73.4 7.3 %collective-permute-done.11.refs_3_.refs_10_.refs_12_.refs_17_ = bf16[640,1024]{1,0:T(8,128)(2,1)S(1)} collective-permute-done((bf16[640,1024]{1,0:T(8,128)(2,1)}, bf16[640,1024]{1,0:T(8,128)(2,1)S(1)}, u32[]{:S(2)}, u32[]{:S(2)}) %collective-permute-start.11) | collective-permute-done | bytes 1310752 | tf_op jit(solution)/shard_map/ppermute | solution.py:1118
  90.8 7.3 %self_2.1 = (bf16[384,1024]{1,0:T(8,128)(2,1)}, bf16[384,1024]{1,0:T(8,128)(2,1)}, bf16[384,1024]{1,0:T(8,128)(2,1)}, bf16[384,1024]{1,0:T(8,128)(2,1)}, bf16[38...) custom-call(s32[3]{0:T(128)} %pad_add_fusion.sc_ref, ...), custom_call_target="tpu_custom_call" | custom-call | flops 27599998976 | tf_op jit(solution)/shard_map/self_2/pallas_call | solution.py:430
  99.9 11.6 %collective-permute-done.14.refs_1_.refs_11_ = bf16[256,1024]{1,0:T(8,128)(2,1)} collective-permute-done((bf16[256,1024]{1,0:T(8,128)(2,1)S(1)}, bf16[256,1024]{1,0:T(8,128)(2,1)}, u32[]{:S(2)}, u32[]{:S(2)}) %collective-permute-start.14) | collective-permute-done | bytes 524320 | tf_op jit(solution)/shard_map/ppermute | solution.py:1112
  111.5 5.5 %collective-permute-done.17.refs_6_.refs_13_.refs_15_.refs_20_ = bf16[320,1024]{1,0:T(8,128)(2,1)S(1)} collective-permute-done((bf16[320,1024]{1,0:T(8,128)(2,1)}, bf16[320,1024]{1,0:T(8,128)(2,1)S(1)}, u32[]{:S(2)}, u32[]{:S(2)}) %collective-permute-start.17) | collective-permute-done | bytes 655392 | tf_op jit(solution)/shard_map/ppermute | solution.py:1118
  121.3 8.7 %mid.1 = (f32[384,1024]{1,0:T(8,128)}, bf16[384,1024]{1,0:T(8,128)(2,1)}, f32[384,1]{1,0:T(8,128)}, bf16[384,32]{1,0:T(8,128)(2,1)}, bf16[384,1024]{1,0:T(8,128)(2,1)}) custom-call(s32[3]{0:T(128)} %pad_add_fusion.sc_ref, bf16[384,1024]{1,0:T(8,128)(2,1)} %get-tuple-element.184.o_ref, bf16[384,1024]{1,0:T(8,128)(2,1)} %bitcast.19, ...), custom_call_target="tpu_custom_call" | custom-call | flops 1150000000 | tf_op jit(solution)/shard_map/mid/pallas_call | solution.py:680
  136.5 23.5 %cross.1 = (bf16[1024,1024]{1,0:T(8,128)(2,1)}, bf16[1024,1024]{1,0:T(8,128)(2,1)}, bf16[1024,32]{1,0:T(8,128)(2,1)}, bf16[1024,16]{1,0:T(8,128)(2,1)}, bf16[384...) custom-call(s32[3]{0:T(128)} %pad_add_fusion.sc_ref, bf16[256,1024]{1,0:T(8,128)(2,1)} %bitcast.43, ...), custom_call_target="tpu_custom_call" | custom-call | flops 36800000000 | tf_op jit(solution)/shard_map/cross/pallas_call | solution.py:430
  160.0 7.3 %mid_cross.1 = (f32[384,1024]{1,0:T(8,128)}, bf16[384,1024]{1,0:T(8,128)(2,1)}, f32[384,1]{1,0:T(8,128)}, bf16[384,16]{1,0:T(8,128)(2,1)}) custom-call(s32[3]{0:T(128)} %pad_add_fusion.sc_ref, bf16[384,1024]{1,0:T(8,128)(2,1)} %get-tuple-element.196.o_ref.oc_in, f32[384,1024]{1,0:T(8,128)} %get-tuple-element.197.x_ref.h1_ref, ...), custom_call_target="tpu_custom_call" | custom-call | flops 1150000000 | tf_op jit(solution)/shard_map/mid_cross/pallas_call | solution.py:680
  172.8 11.8 %gelu_up.1 = (bf16[384,4096]{1,0:T(8,128)(2,1)}, bf16[384,4096]{1,0:T(8,128)(2,1)}, bf16[384,16]{1,0:T(8,128)(2,1)}) custom-call(s32[3]{0:T(128)} %pad_add_fusion.sc_ref, bf16[384,1024]{1,0:T(8,128)(2,1)} %get-tuple-element.200.x_ref.h2_low_in, bf16[1,8,16,1024]{3,2,1,0:T(8,128)(2,1)} %a1_ref.1, bf16[1,8,16,4096]{3,2,1,0:T(8,128)(2,1)} %b1_ref.1, ...), custom_call_target="tpu_custom_call" | custom-call | flops 17250000896 | tf_op jit(solution)/shard_map/gelu_up/pallas_call | solution.py:727
  189.8 32.7 %mlp.1 = (bf16[384,1024]{1,0:T(8,128)(2,1)}, f32[384,1024]{1,0:T(8,128)}, bf16[384,1024]{1,0:T(8,128)(2,1)}, bf16[8,144,768]{2,1,0:T(8,128)(2,1)}, bf16[208,1024]{1,0:T(8,128)(2,1)}) custom-call(s32[3]{0:T(128)} %pad_add_fusion.sc_ref, bf16[384,4096]{1,0:T(8,128)(2,1)} %get-tuple-element.205.g_in, bf16[384,4096]{1,0:T(8,128)(2,1)} %get-tuple-element.206.slope_in, ...), custom_call_target="tpu_custom_call" | custom-call | flops 37950001152 | tf_op jit(solution)/shard_map/mlp/pallas_call | solution.py:852
  222.6 28.4 %cross_back.1 = (f32[256,1024]{1,0:T(8,128)}, bf16[768,1024]{1,0:T(8,128)(2,1)}, bf16[384,1024]{1,0:T(8,128)(2,1)}, bf16[64,1024]{1,0:T(8,128)(2,1)}) custom-call(s32[3]{0:T(128)} %pad_add_fusion.sc_ref, bf16[8,144,768]{2,1,0:T(8,128)(2,1)} %get-tuple-element.217.refs_0_, bf16[8,144,768]{2,1,0:T(8,128)(2,1)} %get-tuple-element.218.refs_1_, ...), custom_call_target="tpu_custom_call" | custom-call | flops 49066668032 | tf_op jit(solution)/shard_map/cross_back/pallas_call | solution.py:607
  256.2 11.0 %mid_back.1 = (f32[384,1024]{1,0:T(8,128)}, bf16[384,1024]{1,0:T(8,128)(2,1)}, bf16[8,144,768]{2,1,0:T(8,128)(2,1)}, bf16[64,1024]{1,0:T(8,128)(2,1)}) custom-call(s32[3]{0:T(128)} %pad_add_fusion.sc_ref, bf16[384,1024]{1,0:T(8,128)(2,1)} %get-tuple-element.224.dqc_ref, f32[384,1024]{1,0:T(8,128)} %get-tuple-element.225.d2_ref, ...), custom_call_target="tpu_custom_call" | custom-call | flops 1150000000 | tf_op jit(solution)/shard_map/mid_back/pallas_call | solution.py:945
  273.1 6.2 %self_back_3.1 = (bf16[384,1024]{1,0:T(8,128)(2,1)}, f32[8,128,384]{2,1,0:T(8,128)}, f32[64,1024]{1,0:T(8,128)}) custom-call(s32[3]{0:T(128)} %pad_add_fusion.sc_ref, bf16[8,144,768]{2,1,0:T(8,128)(2,1)} %get-tuple-element.216.refs_0_, bf16[8,144,768]{2,1,0:T(8,128)(2,1)} %get-tuple-element.231.refs_1_, bf16[384,1024]{1,0:T(8,128)(2,1)} %get-tuple-element.232.refs_2_, ...), custom_call_target="tpu_custom_call" | custom-call | flops 18400000000 | tf_op jit(solution)/shard_map/self_back_3/pallas_call | solution.py:607
  285.0 6.7 %self_back_2.1 = (bf16[384,1024]{1,0:T(8,128)(2,1)}, f32[8,128,384]{2,1,0:T(8,128)}, f32[64,1024]{1,0:T(8,128)}) custom-call(s32[3]{0:T(128)} %pad_add_fusion.sc_ref, bf16[8,144,768]{2,1,0:T(8,128)(2,1)} %get-tuple-element.216.refs_0_, bf16[8,144,768]{2,1,0:T(8,128)(2,1)} %get-tuple-element.231.refs_1_, bf16[384,1024]{1,0:T(8,128)(2,1)} %get-tuple-element.232.refs_2_, ...), custom_call_target="tpu_custom_call" | custom-call | flops 18400000000 | tf_op jit(solution)/shard_map/self_back_2/pallas_call | solution.py:607
  293.1 8.1 %collective-permute-start.32 = (bf16[256,1024]{1,0:T(8,128)(2,1)S(1)}, bf16[256,1024]{1,0:T(8,128)(2,1)}, u32[]{:S(2)}, u32[]{:S(2)}) collective-permute-start(bf16[256,1024]{1,0:T(8,128)(2,1)S(1)} %add_convert_fusion.2), channel_id=1, source_target_pairs={{0,3},{1,0},{2,1},{3,2},{4,7},{5,4},{6,5},{7,6},{8,11},{9,8},{10,9... | collective-permute-start | bytes 1572872 | tf_op jit(solution)/shard_map/ppermute | solution.py:1112
  302.6 6.9 %self_back_1.1 = (bf16[384,1024]{1,0:T(8,128)(2,1)}, f32[8,128,384]{2,1,0:T(8,128)}, f32[64,1024]{1,0:T(8,128)}) custom-call(s32[3]{0:T(128)} %pad_add_fusion.sc_ref, bf16[8,144,768]{2,1,0:T(8,128)(2,1)} %get-tuple-element.216.refs_0_, bf16[8,144,768]{2,1,0:T(8,128)(2,1)} %get-tuple-element.231.refs_1_, bf16[384,1024]{1,0:T(8,128)(2,1)} %get-tuple-element.232.refs_2_, ...), custom_call_target="tpu_custom_call" | custom-call | flops 18400000000 | tf_op jit(solution)/shard_map/self_back_1/pallas_call | solution.py:607
  309.6 5.2 %collective-permute-done.32 = bf16[256,1024]{1,0:T(8,128)(2,1)} collective-permute-done((bf16[256,1024]{1,0:T(8,128)(2,1)S(1)}, bf16[256,1024]{1,0:T(8,128)(2,1)}, u32[]{:S(2)}, u32[]{:S(2)}) %collective-permute-start.32) | collective-permute-done | bytes 524320 | tf_op jit(solution)/shard_map/ppermute | solution.py:1112
  319.1 16.2 %self_back_0.1 = (f32[384,1024]{1,0:T(8,128)}, bf16[96,1024]{1,0:T(8,128)(2,1)}) custom-call(s32[3]{0:T(128)} %pad_add_fusion.sc_ref, bf16[8,144,768]{2,1,0:T(8,128)(2,1)} %get-tuple-element.216.refs_0_, bf16[8,144,768]{2,1,0:T(8,128)(2,1)} %get-tuple-element.231.refs_1_, bf16[384,1024]{1,0:T(8,128)(2,1)} %get-tuple-element.232.refs_2_, ...), custom_call_target="tpu_custom_call" | custom-call | flops 18400000000 | tf_op jit(solution)/shard_map/self_back_0/pallas_call | solution.py:607
  341.6 5.4 %collective-permute-done.35 = bf16[96,1024]{1,0:T(8,128)(2,1)S(1)} collective-permute-done((bf16[96,1024]{1,0:T(8,128)(2,1)}, bf16[96,1024]{1,0:T(8,128)(2,1)S(1)}, u32[]{:S(2)}, u32[]{:S(2)}) %collective-permute-start.35) | collective-permute-done | bytes 196640 | tf_op jit(solution)/shard_map/ppermute | solution.py:1115
  358.3 5.6 %fc_total.1 = (f32[1,8,16,1024]{3,2,1,0:T(8,128)}, f32[1,8,16,4096]{3,2,1,0:T(8,128)}, f32[1,8,16,4096]{3,2,1,0:T(8,128)}, f32[1,8,16,1024]{3,2,1,0:T(8,128)}) custom-call(s32[8]{0:T(128)} %convert_reduce_fusion.picks_ref, bf16[8,208,1024]{2,1,0:T(8,128)(2,1)} %copy-done.5), custom_call_target="tpu_custom_call" | custom-call | flops 6899999744 | tf_op jit(solution)/shard_map/fc_total/pallas_call | solution.py:991
  380.4 6.7 %proj_total_3.1 = (f32[1,8,8,16,1024]{4,3,2,1,0:T(8,128)}, f32[1,8,8,16,1024]{4,3,2,1,0:T(8,128)}) custom-call(s32[8]{0:T(128)} %convert_reduce_fusion.picks_ref, bf16[8,208,1024]{2,1,0:T(8,128)(2,1)} %copy-done.5, bf16[8,128,1024]{2,1,0:T(8,128)(2,1)} %pad_maximum_fusion.3.refs_1_), custom_call_target="tpu_custom_call" | custom-call | flops 8049999872 | tf_op jit(solution)/shard_map/proj_total_3/pallas_call | solution.py:1036
  (194 shorter events, 124.9 us)
Async XLA Ops:
  7.2 165.6 %all-gather.2.cloned.1.call-start = ((), (), s32[]{:S(2)}) async-start(), calls=%async_computation | async-start | bytes 9437184 | tf_op jit(solution)/shard_map/all_gather | solution.py:1126
  9.2 24.5 %collective-permute-start.3 = (bf16[400,1024]{1,0:T(8,128)(2,1)S(1)}, bf16[400,1024]{1,0:T(8,128)(2,1)}, u32[]{:S(2)}, u32[]{:S(2)}) collective-permute-start(bf16[400,1024]{1,0:T(8,128)(2,1)S(1)} %fusion.1.refs_0_.refs_2_.refs_10_), channel_id=1, source_target_pairs={{0,1},{1,2},{2,3},{3,0},{4,5},{5,6},{6,7},{7,4},{8,9},{9,10},{10,1... | collective-permute-start | bytes 2457608 | tf_op jit(solution)/shard_map/ppermute | solution.py:1112
  12.6 20.0 %collective-permute-start.1 = (bf16[384,1024]{1,0:T(8,128)(2,1)S(1)}, bf16[384,1024]{1,0:T(8,128)(2,1)S(1)}, u32[]{:S(2)}, u32[]{:S(2)}) collective-permute-start(bf16[384,1024]{1,0:T(8,128)(2,1)S(1)} %bitcast.23), channel_id=1, source_target_pairs={{0,16},{8,24},{16,0},{24,8},{1,17},{9,25},{17,1},{25,9},{2,18},{10... | collective-permute-start | bytes 2359304 | tf_op jit(solution)/shard_map/ppermute | solution.py:1118
  37.6 21.8 %collective-permute-start.9 = (bf16[400,1024]{1,0:T(8,128)(2,1)}, bf16[400,1024]{1,0:T(8,128)(2,1)}, u32[]{:S(2)}, u32[]{:S(2)}) collective-permute-start(bf16[400,1024]{1,0:T(8,128)(2,1)} %collective-permute-done.3.refs_1_.refs_3_.refs_10_), channel_id=1, source_target_pairs={{0,1},{1,2},{2,3},{3,0},{4,5},{5,6},{6,7},{7,4},{8,9},{9,10},{10,1... | collective-permute-start | bytes 2457608 | tf_op jit(solution)/shard_map/ppermute | solution.py:1112
  49.3 24.1 %collective-permute-start.12 = (bf16[640,1024]{1,0:T(8,128)(2,1)}, bf16[640,1024]{1,0:T(8,128)(2,1)}, u32[]{:S(2)}, u32[]{:S(2)}) collective-permute-start(bf16[640,1024]{1,0:T(8,128)(2,1)} %pad_maximum_fusion.6.refs_0_.refs_7_.refs_9_.refs_14_), channel_id=1, source_target_pairs={{0,4},{4,0},{1,5},{5,1},{2,6},{6,2},{3,7},{7,3},{8,12},{12,8},{9,1... | collective-permute-start | bytes 3932168 | tf_op jit(solution)/shard_map/ppermute | solution.py:1121
  49.3 31.4 %collective-permute-start.11 = (bf16[640,1024]{1,0:T(8,128)(2,1)}, bf16[640,1024]{1,0:T(8,128)(2,1)S(1)}, u32[]{:S(2)}, u32[]{:S(2)}) collective-permute-start(bf16[640,1024]{1,0:T(8,128)(2,1)} %pad_maximum_fusion.6.refs_0_.refs_7_.refs_9_.refs_14_), channel_id=1, source_target_pairs={{0,16},{8,24},{16,0},{24,8},{1,17},{9,25},{17,1},{25,9},{2,18},{10... | collective-permute-start | bytes 3932168 | tf_op jit(solution)/shard_map/ppermute | solution.py:1118
  49.8 31.1 %collective-permute-start.10 = (bf16[640,1024]{1,0:T(8,128)(2,1)}, bf16[640,1024]{1,0:T(8,128)(2,1)S(1)}, u32[]{:S(2)}, u32[]{:S(2)}) collective-permute-start(bf16[640,1024]{1,0:T(8,128)(2,1)} %pad_maximum_fusion.6.refs_0_.refs_7_.refs_9_.refs_14_), channel_id=1, source_target_pairs={{0,8},{8,0},{16,24},{24,16},{1,9},{9,1},{17,25},{25,17},{2,10},{10... | collective-permute-start | bytes 3932168 | tf_op jit(solution)/shard_map/ppermute | solution.py:1118
  59.4 21.5 %collective-permute-start.13 = (bf16[400,1024]{1,0:T(8,128)(2,1)}, bf16[400,1024]{1,0:T(8,128)(2,1)S(1)}, u32[]{:S(2)}, u32[]{:S(2)}) collective-permute-start(bf16[400,1024]{1,0:T(8,128)(2,1)} %collective-permute-done.9.refs_0_.refs_2_.refs_10_), channel_id=1, source_target_pairs={{0,1},{1,2},{2,3},{3,0},{4,5},{5,6},{6,7},{7,4},{8,9},{9,10},{10,1... | collective-permute-start | bytes 2457608 | tf_op jit(solution)/shard_map/ppermute | solution.py:1112
  81.0 190.3 %all-reduce.4.cloned.1.call-start = ((), (), s32[]{:S(2)}) async-start(), calls=%async_computation.1 | async-start | bytes 851968 | tf_op jit(solution)/shard_map/psum | solution.py:1212
  82.8 34.2 %collective-permute-start.18 = (bf16[1280,1024]{1,0:T(8,128)(2,1)}, bf16[1280,1024]{1,0:T(8,128)(2,1)}, u32[]{:S(2)}, u32[]{:S(2)}) collective-permute-start(bf16[1280,1024]{1,0:T(8,128)(2,1)} %pad_maximum_fusion.1), channel_id=1, source_target_pairs={{0,4},{4,0},{1,5},{5,1},{2,6},{6,2},{3,7},{7,3},{8,12},{12,8},{9,1... | collective-permute-start | bytes 7864328 | tf_op jit(solution)/shard_map/ppermute | solution.py:1121
  87.6 23.9 %collective-permute-start.14 = (bf16[256,1024]{1,0:T(8,128)(2,1)S(1)}, bf16[256,1024]{1,0:T(8,128)(2,1)}, u32[]{:S(2)}, u32[]{:S(2)}) collective-permute-start(bf16[256,1024]{1,0:T(8,128)(2,1)S(1)} %bitcast.46), channel_id=1, source_target_pairs={{0,1},{1,2},{2,3},{3,0},{4,5},{5,6},{6,7},{7,4},{8,9},{9,10},{10,1... | collective-permute-start | bytes 1572872 | tf_op jit(solution)/shard_map/ppermute | solution.py:1112
  88.7 28.3 %collective-permute-start.17 = (bf16[320,1024]{1,0:T(8,128)(2,1)}, bf16[320,1024]{1,0:T(8,128)(2,1)S(1)}, u32[]{:S(2)}, u32[]{:S(2)}) collective-permute-start(bf16[320,1024]{1,0:T(8,128)(2,1)} %slice.41), channel_id=1, source_target_pairs={{0,8},{8,0},{16,24},{24,16},{1,9},{9,1},{17,25},{25,17},{2,10},{10... | collective-permute-start | bytes 1966088 | tf_op jit(solution)/shard_map/ppermute | solution.py:1118
  89.2 27.8 %collective-permute-start.16 = (bf16[320,1024]{1,0:T(8,128)(2,1)S(1)}, bf16[320,1024]{1,0:T(8,128)(2,1)S(1)}, u32[]{:S(2)}, u32[]{:S(2)}) collective-permute-start(bf16[320,1024]{1,0:T(8,128)(2,1)S(1)} %slice.40), channel_id=1, source_target_pairs={{0,16},{8,24},{16,0},{24,8},{1,17},{9,25},{17,1},{25,9},{2,18},{10... | collective-permute-start | bytes 1966088 | tf_op jit(solution)/shard_map/ppermute | solution.py:1118
  133.5 33.8 %collective-permute-start.23 = (bf16[512,1024]{1,0:T(8,128)(2,1)}, bf16[512,1024]{1,0:T(8,128)(2,1)S(1)}, u32[]{:S(2)}, u32[]{:S(2)}) collective-permute-start(bf16[512,1024]{1,0:T(8,128)(2,1)} %bitcast.38), channel_id=1, source_target_pairs={{0,4},{4,0},{1,5},{5,1},{2,6},{6,2},{3,7},{7,3},{8,12},{12,8},{9,1... | collective-permute-start | bytes 3145736 | tf_op jit(solution)/shard_map/ppermute | solution.py:1121
  133.5 35.1 %collective-permute-start.22 = (bf16[512,1024]{1,0:T(8,128)(2,1)}, bf16[512,1024]{1,0:T(8,128)(2,1)S(1)}, u32[]{:S(2)}, u32[]{:S(2)}) collective-permute-start(bf16[512,1024]{1,0:T(8,128)(2,1)} %bitcast.39), channel_id=1, source_target_pairs={{0,16},{8,24},{16,0},{24,8},{1,17},{9,25},{17,1},{25,9},{2,18},{10... | collective-permute-start | bytes 3145736 | tf_op jit(solution)/shard_map/ppermute | solution.py:1118
  135.0 33.6 %collective-permute-start.21 = (bf16[512,1024]{1,0:T(8,128)(2,1)}, bf16[512,1024]{1,0:T(8,128)(2,1)S(1)}, u32[]{:S(2)}, u32[]{:S(2)}) collective-permute-start(bf16[512,1024]{1,0:T(8,128)(2,1)} %bitcast.40), channel_id=1, source_target_pairs={{0,8},{8,0},{16,24},{24,16},{1,9},{9,1},{17,25},{25,17},{2,10},{10... | collective-permute-start | bytes 3145736 | tf_op jit(solution)/shard_map/ppermute | solution.py:1118
  222.5 114.8 %all-reduce.6.cloned.1.call-start = ((), (), s32[]{:S(2)}) async-start(), calls=%async_computation.2 | async-start | bytes 524288 | tf_op jit(solution)/shard_map/psum | solution.py:1228
  252.3 27.1 %collective-permute-start.30 = (bf16[256,1024]{1,0:T(8,128)(2,1)S(1)}, bf16[256,1024]{1,0:T(8,128)(2,1)S(1)}, u32[]{:S(2)}, u32[]{:S(2)}) collective-permute-start(bf16[256,1024]{1,0:T(8,128)(2,1)S(1)} %get-tuple-element.313), channel_id=1, source_target_pairs={{0,1},{1,2},{2,3},{3,0},{4,5},{5,6},{6,7},{7,4},{8,9},{9,10},{10,1... | collective-permute-start | bytes 1572872 | tf_op jit(solution)/shard_map/ppermute | solution.py:1112
  253.8 28.4 %collective-permute-start.29 = (bf16[256,1024]{1,0:T(8,128)(2,1)S(1)}, bf16[256,1024]{1,0:T(8,128)(2,1)S(1)}, u32[]{:S(2)}, u32[]{:S(2)}) collective-permute-start(bf16[256,1024]{1,0:T(8,128)(2,1)S(1)} %get-tuple-element.314), channel_id=1, source_target_pairs={{0,3},{1,0},{2,1},{3,2},{4,7},{5,4},{6,5},{7,6},{8,11},{9,8},{10,9... | collective-permute-start | bytes 1572872 | tf_op jit(solution)/shard_map/ppermute | solution.py:1112
  271.4 21.6 %collective-permute-start.28 = (bf16[1,208,1024]{2,1,0:T(8,128)(2,1)}, bf16[1,208,1024]{2,1,0:T(8,128)(2,1)S(1)}, u32[]{:S(2)}, u32[]{:S(2)}) collective-permute-start(bf16[1,208,1024]{2,1,0:T(8,128)(2,1)} %bitcast.34), channel_id=1, source_target_pairs={{0,8},{8,0},{16,24},{24,16},{1,9},{9,1},{17,25},{25,17},{2,10},{10... | collective-permute-start | bytes 1277960 | tf_op jit(solution)/shard_map/ppermute | solution.py:1118
  282.2 27.3 %collective-permute-start.31 = (bf16[384,1024]{1,0:T(8,128)(2,1)}, bf16[384,1024]{1,0:T(8,128)(2,1)S(1)}, u32[]{:S(2)}, u32[]{:S(2)}) collective-permute-start(bf16[384,1024]{1,0:T(8,128)(2,1)} %get-tuple-element.264), channel_id=1, source_target_pairs={{0,3},{1,0},{2,1},{3,2},{4,7},{5,4},{6,5},{7,6},{8,11},{9,8},{10,9... | collective-permute-start | bytes 2359304 | tf_op jit(solution)/shard_map/ppermute | solution.py:1112
  293.1 21.7 %collective-permute-start.32 = (bf16[256,1024]{1,0:T(8,128)(2,1)S(1)}, bf16[256,1024]{1,0:T(8,128)(2,1)}, u32[]{:S(2)}, u32[]{:S(2)}) collective-permute-start(bf16[256,1024]{1,0:T(8,128)(2,1)S(1)} %add_convert_fusion.2), channel_id=1, source_target_pairs={{0,3},{1,0},{2,1},{3,2},{4,7},{5,4},{6,5},{7,6},{8,11},{9,8},{10,9... | collective-permute-start | bytes 1572872 | tf_op jit(solution)/shard_map/ppermute | solution.py:1112
  301.1 34.2 %collective-permute-start.33 = (bf16[2,208,1024]{2,1,0:T(8,128)(2,1)S(1)}, bf16[2,208,1024]{2,1,0:T(8,128)(2,1)S(1)}, u32[]{:S(2)}, u32[]{:S(2)}) collective-permute-start(bf16[2,208,1024]{2,1,0:T(8,128)(2,1)S(1)} %pad_maximum_fusion.10), channel_id=1, source_target_pairs={{0,16},{8,24},{16,0},{24,8},{1,17},{9,25},{17,1},{25,9},{2,18},{10... | collective-permute-start | bytes 2555912 | tf_op jit(solution)/shard_map/ppermute | solution.py:1118
  316.0 23.6 %collective-permute-start.34 = (bf16[384,1024]{1,0:T(8,128)(2,1)}, bf16[384,1024]{1,0:T(8,128)(2,1)}, u32[]{:S(2)}, u32[]{:S(2)}) collective-permute-start(bf16[384,1024]{1,0:T(8,128)(2,1)} %add_convert_fusion.1), channel_id=1, source_target_pairs={{0,3},{1,0},{2,1},{3,2},{4,7},{5,4},{6,5},{7,6},{8,11},{9,8},{10,9... | collective-permute-start | bytes 2359304 | tf_op jit(solution)/shard_map/ppermute | solution.py:1112
  (58 other events, 479.2 us)
Sparse Core Ops, SparseCore 0:
  81.1 76.4 all-gather.1
  222.6 48.6 all-reduce.3
  273.8 63.5 all-reduce.5
